TPU v7x, 512 devices: a whole 4x8x8 slice. The times are simulated.
512 devices in a mesh: gx: 32 (over z, x), gy: 16 (over y, core).
Axes of the slice: x: 4, y: 8, z: 8, core: 2. Of those that a mesh axis runs over, the one named last changes fastest.
Arguments:
- source: float32 [5, 4, 4, 4, 64, 32, 128], P(None, None, None, None, 'gx', 'gy'), may hold values from -18 to 18
- jacobian: float32 [3, 5, 5, 64, 32, 128], P(None, None, None, 'gx', 'gy'), may hold values from -1.8 to 1.8
- damping: float32 [64, 32, 128], P('gx', 'gy'), may hold values from 0.3 to 1.2
- orient: int32 [3, 64, 32, 128], P(None, 'gx', 'gy'), may hold values 0 or 1
- smoother: bfloat16 [5, 5, 4, 4, 4, 64, 32, 128], P(None, None, None, None, None, 'gx', 'gy'), may hold values from -0.4 to 0.4, as said below
- coarse_smoother: bfloat16 [5, 5, 2, 2, 2, 64, 32, 128], P(None, None, None, None, None, 'gx', 'gy'), may hold values from -0.61 to 1.11, as said below
Outputs:
- corrected: float32 [5, 4, 4, 4, 64, 32, 128], P(None, None, None, None, 'gx', 'gy')
Inputs may be any that keep to these rules, and one draw needn't show every extreme that they name: `smoother`: each 5 x 5 block is a positive node scale times the identity plus independent entries. `coarse_smoother`: each 5 x 5 block is a positive node scale times the identity plus independent entries.
All inputs are finite; a program needn't handle non-finite values. No bound on the sum of `orient` on one device may be relied on, other than what follows from the above.
Results may differ from a plain program's by a relative error of at most 0.0003.
Values sent between devices are 32-bit elements; how exact they have to be, the bound alone decides.
A program may use at most 64 MiB of HBM per device.

v0:
```python
import functools
import math

import jax
import jax.numpy as jnp
import numpy as np
from jax import lax
from jax.experimental import pallas as pl
from jax.experimental.pallas import tpu as pltpu
from jax.sharding import PartitionSpec as P

MESH = pl.DeviceIdType.MESH
OMEGA = 0.8
SHIFT = 2.0
F32 = jnp.float32


def lobatto4():
    points = np.array([-1.0, -1.0 / math.sqrt(5.0), 1.0 / math.sqrt(5.0), 1.0])
    weights = np.ones(4)
    for row in range(4):
        for col in range(4):
            if row != col:
                weights[row] /= points[row] - points[col]
    slopes = np.zeros((4, 4))
    for row in range(4):
        for col in range(4):
            if row != col:
                slopes[row, col] = weights[col] / weights[row] / (points[row] - points[col])
        slopes[row, row] = -np.sum(slopes[row])
    return points, slopes


POINTS, SLOPES = lobatto4()
INTERP = np.stack([(1.0 - POINTS) / 2.0, (1.0 + POINTS) / 2.0], 1)
OPEN = SLOPES.copy()
OPEN[0, 0] = OPEN[3, 3] = OPEN[1, 1] = OPEN[2, 2] = 0.0
LIFT = 3.0
EDGE = INTERP.T @ OPEN
P_NEAR, P_FAR = float(INTERP[1, 0]), float(INTERP[2, 0])


def dot_terms(coefs, values):
    total = None
    for coef, value in zip(coefs, values):
        coef = float(coef)
        if coef == 0.0:
            continue
        term = value if coef == 1.0 else coef * value
        total = term if total is None else total + term
    return total


def rows():
    return lax.broadcasted_iota(jnp.int32, (8, 128), 0)


def halves(top, bottom):
    return jnp.where(rows() < 4, jnp.full((8, 128), float(top), F32), jnp.full((8, 128), float(bottom), F32))


def sub_roll(value, shift):
    return pltpu.roll(value, shift % 8, 0)


def lane_roll(value, shift):
    return pltpu.roll(value, shift % 128, 1)


def pack_low(first, second, mask, step):
    return jnp.where(mask, first, sub_roll(second, step))


def pack_high(first, second, mask, step):
    return jnp.where(mask, sub_roll(first, -step), second)


def z_ghosts(traces, turned):
    count = len(traces)
    low = rows() < 4
    flip = jnp.logical_and(turned, rows() >= 4)
    out = []
    for a in range(count):
        swapped = sub_roll(jnp.where(flip, traces[count - 1 - a], traces[a]), 4)
        out.append(jnp.where(low, lane_roll(swapped, 1), lane_roll(swapped, -1)))
    return [jnp.where(flip, out[count - 1 - a], out[a]) for a in range(count)]


def restrict_c(first, second):
    low = rows() < 4
    ends = jnp.where(low, first, second)
    inner_swapped = jnp.where(low, second, first)
    inner = sub_roll(inner_swapped, 4)
    return ends, inner, inner_swapped, ends + P_NEAR * inner + P_FAR * inner_swapped


def restrict_line(values):
    low = values[0] + P_NEAR * values[1] + P_FAR * values[2]
    high = values[3] + P_NEAR * values[2] + P_FAR * values[1]
    return [low, high]


def prolong_line(values):
    return [
        values[0],
        P_NEAR * values[0] + P_FAR * values[1],
        P_FAR * values[0] + P_NEAR * values[1],
        values[1],
    ]


def kernel(
    src_hbm, jac_hbm, damp_hbm, flag_hbm, smo_hbm, csm_hbm, out_hbm,
    src, smo, csm, jraw, jn, draw, fraw, flags, dmp, kfine, csf,
    q, acc, wx, wy, wz, rsrc, rcs, ctr, wc, cfield, crhs,
    s1, r1, s2, r2, in_sem, out_sem, send_sem, recv_sem,
):
    nx, ny = lax.axis_size("gx"), lax.axis_size("gy")
    ix, iy = lax.axis_index("gx"), lax.axis_index("gy")
    x_next, x_prev = lax.rem(ix + 1, nx), lax.rem(ix + nx - 1, nx)
    y_next, y_prev = lax.rem(iy + 1, ny), lax.rem(iy + ny - 1, ny)
    partners = [(x_prev, iy), (x_next, iy), (ix, y_prev), (ix, y_next)]

    loads = []

    def load(source, target):
        copy = pltpu.make_async_copy(source, target, in_sem.at[len(loads)])
        copy.start()
        loads.append(copy)
        return copy

    parts = {}
    for a in (0, 3):
        parts[a] = (load(src_hbm.at[:, a], src.at[:, a]), load(smo_hbm.at[:, a], smo.at[:, a]))
    flag_load = load(flag_hbm, fraw)
    damp_load = load(damp_hbm, draw)
    jac_load = load(jac_hbm, jraw)
    for a in (1, 2):
        parts[a] = (load(src_hbm.at[:, a], src.at[:, a]), load(smo_hbm.at[:, a], smo.at[:, a]))
    csm_load = load(csm_hbm, csm)

    barrier = pltpu.get_barrier_semaphore()
    for partner in partners:
        pl.semaphore_signal(barrier, inc=1, device_id=partner, device_id_type=MESH)

    def remote(source, target, number, partner):
        return pltpu.make_async_remote_copy(
            src_ref=source, dst_ref=target, send_sem=send_sem.at[number], recv_sem=recv_sem.at[number],
            device_id=partner, device_id_type=MESH,
        )

    sends1 = [remote(s1.at[k], r1.at[k], k, partners[k]) for k in range(4)]
    sends2 = [[remote(s2.at[r, k], r2.at[r, k], 4 + 4 * r + k, partners[k]) for k in range(4)] for r in range(3)]

    low = rows() < 4
    x0 = (rows() & 2) == 0
    y0 = (rows() & 1) == 0

    def turned(direction):
        return flags[direction] == 1

    def smooth(a, b, fields):
        outs = []
        for vo in range(5):
            pair = [None, None]
            for vi in range(5):
                block = smo[5 * vo + vi, a, b].astype(F32)
                for half in range(2):
                    term = block[8 * half : 8 * half + 8] * fields[vi][half]
                    pair[half] = term if vi == 0 else pair[half] + term
            outs.append(pair)
        return outs

    def first_pass(a, b):
        fields = [[src[v, a, b, 0], src[v, a, b, 1]] for v in range(5)]
        outs = smooth(a, b, fields)
        for v in range(5):
            q[v, a, b, 0] = outs[v][0]
            q[v, a, b, 1] = outs[v][1]

    for a in (0, 3):
        for copy in parts[a]:
            copy.wait()

        @pl.loop(0, 4)
        def _(b, a=a):
            first_pass(a, b)

    flag_load.wait()
    damp_load.wait()
    for d in range(3):
        flags[d] = jnp.concatenate([fraw[d], fraw[d]], axis=0)
    damping = jnp.concatenate([draw[...], draw[...]], axis=0)
    dmp[0] = (OMEGA * LIFT) * damping
    dmp[1] = (OMEGA * 0.5) * damping
    dmp[2] = OMEGA * SHIFT + (OMEGA * 1.5) * damping
    dmp[3] = jnp.where(low, (OMEGA * LIFT) * damping, 0.0)
    dmp[4] = jnp.where(low, 0.0, (OMEGA * LIFT) * damping)
    for b in range(4):
        for a_end in range(2):
            faces = a_end + (1 if b in (0, 3) else 0)
            base = OMEGA * SHIFT + (OMEGA * LIFT * faces) * damping
            kfine[b, a_end, 0] = base + dmp[3]
            kfine[b, a_end, 1] = base + dmp[4]

    fx, fy, fz = turned(0), turned(1), turned(2)

    @pl.loop(0, 5)
    def _(v):
        for b in range(4):
            s1[0, v, b] = pack_low(q[v, 0, b, 0], q[v, 0, b, 1], x0, 2)
            hi = [jnp.where(fx, q[v, 3, 3 - b, h], q[v, 3, b, h]) for h in range(2)]
            s1[1, v, b] = pack_high(hi[0], hi[1], x0, 2)

    pl.semaphore_wait(barrier, 4)
    sends1[0].start()
    sends1[1].start()

    for a in (1, 2):
        for copy in parts[a]:
            copy.wait()

        @pl.loop(0, 4)
        def _(b, a=a):
            first_pass(a, b)

    @pl.loop(0, 5)
    def _(v):
        for a in range(4):
            s1[2, v, a] = pack_low(q[v, a, 0, 0], q[v, a, 0, 1], y0, 1)
            hi = [jnp.where(fy, q[v, 3 - a, 3, h], q[v, a, 3, h]) for h in range(2)]
            s1[3, v, a] = pack_high(hi[0], hi[1], y0, 1)

    sends1[2].start()
    sends1[3].start()

    jac_load.wait()

    @pl.loop(0, 75)
    def _(i):
        block = jraw[i]
        jn[i] = (-OMEGA) * jnp.concatenate([block, block], axis=0)

    csm_load.wait()

    @pl.loop(0, 25)
    def _(i):
        for n in range(2):
            block = csm[i, n].astype(F32)
            csf[i, n, 0] = block[:8]
            csf[i, n, 1] = block[8:]

    c_first = [halves(OPEN[0, 1], OPEN[1, 0]), halves(OPEN[0, 2], OPEN[1, 3]), halves(OPEN[0, 3], OPEN[1, 2])]
    c_second = [halves(OPEN[2, 3], OPEN[3, 2]), halves(OPEN[2, 0], OPEN[3, 1]), halves(OPEN[2, 1], OPEN[3, 0])]
    c_ghost = [halves(-LIFT, 0.0), halves(0.0, LIFT)]

    @pl.loop(0, 20)
    def _(t):
        v, b = t // 4, t % 4
        first = [q[v, a, b, 0] for a in range(4)]
        second = [q[v, a, b, 1] for a in range(4)]
        for a in range(4):
            for h, line in enumerate((first, second)):
                wx[v, a, b, h] = dot_terms(OPEN[a], line)
        ghosts = z_ghosts([jnp.where(low, first[a], second[a]) for a in range(4)], fz)
        for a in range(4):
            a_end = 1 if a in (0, 3) else 0
            first_sw, second_sw = sub_roll(first[a], 4), sub_roll(second[a], 4)
            wz[v, a, b, 0] = (
                c_first[0] * first_sw + c_first[1] * second[a] + c_first[2] * second_sw + c_ghost[0] * ghosts[a]
            )
            wz[v, a, b, 1] = (
                c_second[0] * second_sw + c_second[1] * first[a] + c_second[2] * first_sw + c_ghost[1] * ghosts[a]
            )
            acc[v, a, b, 0] = src[v, a, b, 0] - kfine[b, a_end, 0] * first[a] + dmp[3] * ghosts[a]
            acc[v, a, b, 1] = src[v, a, b, 1] - kfine[b, a_end, 1] * second[a] + dmp[4] * ghosts[a]

    @pl.loop(0, 20)
    def _(t):
        v, a = t // 4, t % 4
        for h in range(2):
            line = [q[v, a, b, h] for b in range(4)]
            for b in range(4):
                wy[v, a, b, h] = dot_terms(OPEN[b], line)

    @pl.loop(0, 5)
    def _(v):
        by_a = []
        for a in range(4):
            by_a.append(restrict_line([restrict_c(src[v, a, b, 0], src[v, a, b, 1])[3] for b in range(4)]))
        for j in range(2):
            for i, value in enumerate(restrict_line([by_a[a][j] for a in range(4)])):
                rsrc[v, i, j] = value

    lift_damp = dmp[0]

    sends1[2].wait_recv()
    sends1[3].wait_recv()

    @pl.loop(0, 5)
    def _(v):
        for h in range(2):
            lo = [q[v, a, 0, h] for a in range(4)]
            hi = [q[v, a, 3, h] for a in range(4)]
            right = []
            for a in range(4):
                packed = r1[2, v, a]
                right.append(jnp.where(y0, sub_roll(lo[a], -1), sub_roll(packed, 1) if h == 0 else packed))
            for a in range(4):
                packed = r1[3, v, a]
                hi_turned = jnp.where(fy, hi[3 - a], hi[a])
                left = jnp.where(y0, packed if h == 0 else sub_roll(packed, -1), sub_roll(hi_turned, 1))
                ghost = jnp.where(fy, right[3 - a], right[a])
                wy[v, a, 0, h] = wy[v, a, 0, h] - LIFT * left
                wy[v, a, 3, h] = wy[v, a, 3, h] + LIFT * ghost
                acc[v, a, 0, h] = acc[v, a, 0, h] + lift_damp * left
                acc[v, a, 3, h] = acc[v, a, 3, h] + lift_damp * ghost

    sends1[0].wait_recv()
    sends1[1].wait_recv()

    @pl.loop(0, 5)
    def _(v):
        for h in range(2):
            lo = [q[v, 0, b, h] for b in range(4)]
            hi = [q[v, 3, b, h] for b in range(4)]
            right = []
            for b in range(4):
                packed = r1[0, v, b]
                right.append(jnp.where(x0, sub_roll(lo[b], -2), sub_roll(packed, 2) if h == 0 else packed))
            for b in range(4):
                packed = r1[1, v, b]
                hi_turned = jnp.where(fx, hi[3 - b], hi[b])
                left = jnp.where(x0, packed if h == 0 else sub_roll(packed, -2), sub_roll(hi_turned, 2))
                ghost = jnp.where(fx, right[3 - b], right[b])
                wx[v, 0, b, h] = wx[v, 0, b, h] - LIFT * left
                wx[v, 3, b, h] = wx[v, 3, b, h] + LIFT * ghost
                acc[v, 0, b, h] = acc[v, 0, b, h] + lift_damp * left
                acc[v, 3, b, h] = acc[v, 3, b, h] + lift_damp * ghost

    @pl.loop(0, 8)
    def _(t):
        half, b = t // 4, t % 4
        pair = [half, 3 - half]
        total = [[[acc[v, a, b, h] for h in range(2)] for a in pair] for v in range(5)]
        for d, w in enumerate((wx, wy, wz)):
            for vi in range(5):
                flux = [[w[vi, a, b, h] for h in range(2)] for a in pair]
                for vo in range(5):
                    weight = jn[25 * d + 5 * vo + vi]
                    for n in range(2):
                        for h in range(2):
                            total[vo][n][h] = total[vo][n][h] + weight * flux[n][h]
        for n, a in enumerate(pair):
            outs = smooth(a, b, [total[v][n] for v in range(5)])
            for v in range(5):
                for h in range(2):
                    q[v, a, b, h] = q[v, a, b, h] + outs[v][h]

    def send_coarse(level):
        @pl.loop(0, 5)
        def _(v):
            s2[level, 0, v] = pack_low(ctr[0, v, 0], ctr[0, v, 1], x0, 2)
            hi = [jnp.where(fx, ctr[1, v, 1 - j], ctr[1, v, j]) for j in range(2)]
            s2[level, 1, v] = pack_high(hi[0], hi[1], x0, 2)
            s2[level, 2, v] = pack_low(ctr[2, v, 0], ctr[2, v, 1], y0, 1)
            hi = [jnp.where(fy, ctr[3, v, 1 - i], ctr[3, v, i]) for i in range(2)]
            s2[level, 3, v] = pack_high(hi[0], hi[1], y0, 1)

        for copy in sends2[level]:
            copy.start()

    def coarse_ghosts(level, v, slot, mask, step, flip):
        lo = [ctr[slot, v, n] for n in range(2)]
        hi = [ctr[slot + 1, v, n] for n in range(2)]
        packed_lo, packed_hi = r2[level, slot, v], r2[level, slot + 1, v]
        right = [
            jnp.where(mask, sub_roll(lo[0], -step), sub_roll(packed_lo, step)),
            jnp.where(mask, sub_roll(lo[1], -step), packed_lo),
        ]
        right = [jnp.where(flip, right[1 - n], right[n]) for n in range(2)]
        hi = [jnp.where(flip, hi[1 - n], hi[n]) for n in range(2)]
        left = [
            jnp.where(mask, packed_hi, sub_roll(hi[0], step)),
            jnp.where(mask, sub_roll(packed_hi, -step), sub_roll(hi[1], step)),
        ]
        return left, right

    def coarse_mix():
        total = [[[crhs[1, v, i, j] for j in range(2)] for i in range(2)] for v in range(5)]
        for d in range(3):
            for vi in range(5):
                flux = [[wc[d, vi, i, j] for j in range(2)] for i in range(2)]
                for vo in range(5):
                    weight = jn[25 * d + 5 * vo + vi]
                    for i in range(2):
                        for j in range(2):
                            total[vo][i][j] = total[vo][i][j] + weight * flux[i][j]
        return total

    def coarse_smooth(total):
        outs = [[[None, None] for _ in range(2)] for _ in range(5)]
        for vo in range(5):
            for vi in range(5):
                for i in range(2):
                    for j in range(2):
                        term = csf[5 * vo + vi, i, j] * total[vi][i][j]
                        outs[vo][i][j] = term if vi == 0 else outs[vo][i][j] + term
        return outs

    @pl.loop(0, 5)
    def _(v):
        rc = [[restrict_c(q[v, a, b, 0], q[v, a, b, 1])[3] for b in range(4)] for a in range(4)]
        rbc = [restrict_line(rc[a]) for a in range(4)]
        rac = [restrict_line([rc[a][b] for a in range(4)]) for b in range(4)]
        for n in range(2):
            ctr[0, v, n] = rbc[0][n]
            ctr[1, v, n] = rbc[3][n]
            ctr[2, v, n] = rac[0][n]
            ctr[3, v, n] = rac[3][n]
        for i in range(2):
            for j in range(2):
                wc[0, v, i, j] = dot_terms(EDGE[i], [rbc[a][j] for a in range(4)])
                wc[1, v, i, j] = dot_terms(EDGE[j], [rac[b][i] for b in range(4)])

    send_coarse(0)

    e_ends = halves(EDGE[0, 0], EDGE[1, 3])
    e_ends_sw = halves(EDGE[0, 3], EDGE[1, 0])
    e_inner = halves(EDGE[0, 1], EDGE[1, 2])
    e_inner_sw = halves(EDGE[0, 2], EDGE[1, 1])
    z_lift = halves(-LIFT, LIFT)

    @pl.loop(0, 5)
    def _(v):
        ra = [[restrict_line([q[v, a, b, h] for a in range(4)]) for b in range(4)] for h in range(2)]
        traces = [[None, None], [None, None]]
        for i in range(2):
            first = restrict_line([ra[0][b][i] for b in range(4)])
            second = restrict_line([ra[1][b][i] for b in range(4)])
            for j in range(2):
                ends, inner, inner_sw, full = restrict_c(first[j], second[j])
                traces[j][i] = ends
                wc[2, v, i, j] = (
                    e_ends * ends + e_ends_sw * sub_roll(ends, 4) + e_inner * inner + e_inner_sw * inner_sw
                )
                crhs[1, v, i, j] = rsrc[v, i, j] - (OMEGA * SHIFT) * full
        for j in range(2):
            ghosts = z_ghosts(traces[j], fz)
            for i in range(2):
                wc[2, v, i, j] = wc[2, v, i, j] + z_lift * ghosts[i]
                crhs[1, v, i, j] = crhs[1, v, i, j] + lift_damp * (ghosts[i] - traces[j][i])

    for copy in sends2[0]:
        copy.wait_recv()

    @pl.loop(0, 5)
    def _(v):
        left, right = coarse_ghosts(0, v, 0, x0, 2, fx)
        for j in range(2):
            wc[0, v, 0, j] = wc[0, v, 0, j] - LIFT * left[j]
            wc[0, v, 1, j] = wc[0, v, 1, j] + LIFT * right[j]
            crhs[1, v, 0, j] = crhs[1, v, 0, j] + lift_damp * (left[j] - ctr[0, v, j])
            crhs[1, v, 1, j] = crhs[1, v, 1, j] + lift_damp * (right[j] - ctr[1, v, j])
        left, right = coarse_ghosts(0, v, 2, y0, 1, fy)
        for i in range(2):
            wc[1, v, i, 0] = wc[1, v, i, 0] - LIFT * left[i]
            wc[1, v, i, 1] = wc[1, v, i, 1] + LIFT * right[i]
            crhs[1, v, i, 0] = crhs[1, v, i, 0] + lift_damp * (left[i] - ctr[2, v, i])
            crhs[1, v, i, 1] = crhs[1, v, i, 1] + lift_damp * (right[i] - ctr[3, v, i])

    total = coarse_mix()
    for v in range(5):
        for i in range(2):
            for j in range(2):
                crhs[0, v, i, j] = total[v][i][j]
    outs = coarse_smooth(total)
    for v in range(5):
        for i in range(2):
            for j in range(2):
                cfield[v, i, j] = outs[v][i][j]

    half_damp, k_coarse = dmp[1], dmp[2]

    for level in (1, 2):
        @pl.loop(0, 5)
        def _(v):
            for n in range(2):
                ctr[0, v, n] = cfield[v, 0, n]
                ctr[1, v, n] = cfield[v, 1, n]
                ctr[2, v, n] = cfield[v, n, 0]
                ctr[3, v, n] = cfield[v, n, 1]

        send_coarse(level)

        @pl.loop(0, 5)
        def _(v):
            for j in range(2):
                field = [cfield[v, i, j] for i in range(2)]
                ghosts = z_ghosts(field, fz)
                for i in range(2):
                    swapped = sub_roll(field[i], 4)
                    wc[2, v, i, j] = jnp.where(low, 0.5, -0.5) * (swapped - ghosts[i])
                    crhs[1, v, i, j] = crhs[0, v, i, j] - k_coarse * field[i] + half_damp * ghosts[i]

        for copy in sends2[level]:
            copy.wait_recv()

        @pl.loop(0, 5)
        def _(v):
            left, right = coarse_ghosts(level, v, 0, x0, 2, fx)
            for j in range(2):
                wc[0, v, 0, j] = 0.5 * (cfield[v, 1, j] - left[j])
                wc[0, v, 1, j] = 0.5 * (right[j] - cfield[v, 0, j])
                crhs[1, v, 0, j] = crhs[1, v, 0, j] + half_damp * left[j]
                crhs[1, v, 1, j] = crhs[1, v, 1, j] + half_damp * right[j]
            left, right = coarse_ghosts(level, v, 2, y0, 1, fy)
            for i in range(2):
                wc[1, v, i, 0] = 0.5 * (cfield[v, i, 1] - left[i])
                wc[1, v, i, 1] = 0.5 * (right[i] - cfield[v, i, 0])
                crhs[1, v, i, 0] = crhs[1, v, i, 0] + half_damp * left[i]
                crhs[1, v, i, 1] = crhs[1, v, i, 1] + half_damp * right[i]

        outs = coarse_smooth(coarse_mix())
        for v in range(5):
            for i in range(2):
                for j in range(2):
                    cfield[v, i, j] = cfield[v, i, j] + outs[v][i][j]

    t_first = [halves(OMEGA, OMEGA * P_FAR), halves(0.0, OMEGA * P_NEAR)]
    t_second = [halves(OMEGA * P_FAR, OMEGA), halves(OMEGA * P_NEAR, 0.0)]

    @pl.loop(0, 5)
    def _(v):
        by_a = [prolong_line([cfield[v, i, j] for i in range(2)]) for j in range(2)]
        for a in range(4):
            for b, value in enumerate(prolong_line([by_a[j][a] for j in range(2)])):
                swapped = sub_roll(value, 4)
                wx[v, a, b, 0] = OMEGA * q[v, a, b, 0] + (t_first[0] * value + t_first[1] * swapped)
                wx[v, a, b, 1] = OMEGA * q[v, a, b, 1] + (t_second[0] * value + t_second[1] * swapped)

    store = pltpu.make_async_copy(wx, out_hbm, out_sem)
    store.start()
    for copy in sends1:
        copy.wait_send()
    for level in sends2:
        for copy in level:
            copy.wait_send()
    store.wait()


def body(source, jacobian, damping, orient, smoother, coarse_smoother):
    field = (5, 4, 4, 2, 8, 128)
    any_space = pl.BlockSpec(memory_space=pl.ANY)
    vmem = pltpu.VMEM
    out = pl.pallas_call(
        kernel,
        out_shape=jax.ShapeDtypeStruct(field, F32),
        in_specs=[any_space] * 6,
        out_specs=any_space,
        scratch_shapes=[
            vmem(field, F32),
            vmem((25, 4, 4, 16, 128), jnp.bfloat16),
            vmem((25, 2, 16, 128), jnp.bfloat16),
            vmem((75, 4, 128), F32),
            vmem((75, 8, 128), F32),
            vmem((4, 128), F32),
            vmem((3, 4, 128), jnp.int32),
            vmem((3, 8, 128), jnp.int32),
            vmem((5, 8, 128), F32),
            vmem((4, 2, 2, 8, 128), F32),
            vmem((25, 2, 2, 8, 128), F32),
            vmem(field, F32),
            vmem(field, F32),
            vmem(field, F32),
            vmem(field, F32),
            vmem(field, F32),
            vmem((5, 2, 2, 8, 128), F32),
            vmem((8, 128), F32),
            vmem((4, 5, 2, 8, 128), F32),
            vmem((3, 5, 2, 2, 8, 128), F32),
            vmem((5, 2, 2, 8, 128), F32),
            vmem((2, 5, 2, 2, 8, 128), F32),
            vmem((4, 5, 4, 8, 128), F32),
            vmem((4, 5, 4, 8, 128), F32),
            vmem((3, 4, 5, 8, 128), F32),
            vmem((3, 4, 5, 8, 128), F32),
            pltpu.SemaphoreType.DMA((12,)),
            pltpu.SemaphoreType.DMA,
            pltpu.SemaphoreType.DMA((16,)),
            pltpu.SemaphoreType.DMA((16,)),
        ],
        compiler_params=pltpu.CompilerParams(
            collective_id=0, has_side_effects=True, vmem_limit_bytes=40 * 1024 * 1024
        ),
    )(
        source.reshape(field),
        jacobian.reshape(75, 4, 128),
        damping.reshape(4, 128),
        orient.reshape(3, 4, 128),
        smoother.reshape(25, 4, 4, 16, 128),
        coarse_smoother.reshape(25, 2, 16, 128),
    )
    return out.reshape(5, 4, 4, 4, 2, 2, 128)


def solution(mesh):
    in_specs = (
        P(None, None, None, None, "gx", "gy", None),
        P(None, None, None, "gx", "gy", None),
        P("gx", "gy", None),
        P(None, "gx", "gy", None),
        P(None, None, None, None, None, "gx", "gy", None),
        P(None, None, None, None, None, "gx", "gy", None),
    )
    out_specs = P(None, None, None, None, "gx", "gy", None)
    return jax.shard_map(body, mesh=mesh, in_specs=in_specs, out_specs=out_specs, check_vma=False)
```

profile of v0, /device:TPU:56, one launch (start us, length us, event | category | flops | bytes accessed | tf_op | source)
XLA Modules:
  0.0 40.6 jit_solution(9829862453713900577)
XLA Ops:
  0.0 0.0 copy-start
  0.0 1.4 %copy-done = bf16[5,5,4,4,4,2,2,128]{7,6,5,4,3,2,1,0:T(2,128)(2,1)S(1)} copy-done((bf16[5,5,4,4,4,2,2,128]{7,6,5,4,3,2,1,0:T(2,128)(2,1)S(1)}, bf16[5,5,4,4,4,2,2,128]{7,6,5,4,3,2,1,0:T(2,128)(2,1)}, u32[]{:S(2)}) %copy-start) | copy-done | bytes 1638424
  1.4 0.0 copy-start.1
  1.4 1.1 %copy-done.1 = f32[5,4,4,4,2,2,128]{6,5,4,3,2,1,0:T(2,128)S(1)} copy-done((f32[5,4,4,4,2,2,128]{6,5,4,3,2,1,0:T(2,128)S(1)}, f32[5,4,4,4,2,2,128]{6,5,4,3,2,1,0:T(2,128)}, u32[]{:S(2)}) %copy-start.1) | copy-done | bytes 655384
  2.5 0.0 copy-start.2
  2.5 0.9 %copy-done.2 = bf16[5,5,2,2,2,2,2,128]{7,6,5,4,3,2,1,0:T(2,128)(2,1)S(1)} copy-done((bf16[5,5,2,2,2,2,2,128]{7,6,5,4,3,2,1,0:T(2,128)(2,1)S(1)}, bf16[5,5,2,2,2,2,2,128]{7,6,5,4,3,2,1,0:T(2,128)(2,1)}, u32[]{:S(2)}) %copy-start.2) | copy-done | bytes 204824
  3.5 0.0 copy-start.3
  3.5 0.9 %copy-done.3 = f32[3,5,5,2,2,128]{5,4,3,2,1,0:T(2,128)S(1)} copy-done((f32[3,5,5,2,2,128]{5,4,3,2,1,0:T(2,128)S(1)}, f32[3,5,5,2,2,128]{5,4,3,2,1,0:T(2,128)}, u32[]{:S(2)}) %copy-start.3) | copy-done | bytes 153624
  4.4 0.0 copy-start.4
  4.4 0.7 %copy-done.4 = s32[3,2,2,128]{3,2,1,0:T(2,128)S(1)} copy-done((s32[3,2,2,128]{3,2,1,0:T(2,128)S(1)}, s32[3,2,2,128]{3,2,1,0:T(2,128)}, u32[]{:S(2)}) %copy-start.4) | copy-done | bytes 6168
  5.1 0.0 copy-start.5
  5.1 0.7 %copy-done.5 = f32[2,2,128]{2,1,0:T(2,128)S(1)} copy-done((f32[2,2,128]{2,1,0:T(2,128)S(1)}, f32[2,2,128]{2,1,0:T(2,128)}, u32[]{:S(2)}) %copy-start.5) | copy-done | bytes 2072
  5.7 34.0 %shard_map.64 = f32[5,4,4,2,8,128]{5,4,3,2,1,0:T(8,128)S(1)} custom-call(f32[5,4,4,2,8,128]{5,4,3,2,1,0:T(8,128)S(1)} %bitcast.9, f32[75,4,128]{2,1,0:T(4,128)S(1)} %bitcast.11, f32[4,128]{1,0:T(4,128)S(1)} %bitcast.13, s32[3,4,128]{2,1,0:T(4,128)S(1)} %bitcast.12, bf16[25,4,4,16,128]{4,3,2,1,0:T(8,128)(2,1)S(1)} %bitcast.8, ...), custom_call_target="tpu_custom_call" | custom-call | tf_op jit(solution)/shard_map/pallas_call | solution.py:556
  39.7 0.8 %copy.8 = f32[5,4,4,4,2,2,128]{6,5,4,3,2,1,0:T(2,128)} copy(f32[5,4,4,4,2,2,128]{6,5,4,3,2,1,0:T(2,128)S(1)} %bitcast.7) | data formatting | bytes 1310720
Async XLA Ops:
  0.0 1.4 %copy-start = (bf16[5,5,4,4,4,2,2,128]{7,6,5,4,3,2,1,0:T(2,128)(2,1)S(1)}, bf16[5,5,4,4,4,2,2,128]{7,6,5,4,3,2,1,0:T(2,128)(2,1)}, u32[]{:S(2)}) copy-start(bf16[5,5,4,4,4,2,2,128]{7,6,5,4,3,2,1,0:T(2,128)(2,1)} %param.10) | copy-start | bytes 4915204
  1.4 1.1 %copy-start.1 = (f32[5,4,4,4,2,2,128]{6,5,4,3,2,1,0:T(2,128)S(1)}, f32[5,4,4,4,2,2,128]{6,5,4,3,2,1,0:T(2,128)}, u32[]{:S(2)}) copy-start(f32[5,4,4,4,2,2,128]{6,5,4,3,2,1,0:T(2,128)} %param.6) | copy-start | bytes 1966084
  2.5 0.9 %copy-start.2 = (bf16[5,5,2,2,2,2,2,128]{7,6,5,4,3,2,1,0:T(2,128)(2,1)S(1)}, bf16[5,5,2,2,2,2,2,128]{7,6,5,4,3,2,1,0:T(2,128)(2,1)}, u32[]{:S(2)}) copy-start(bf16[5,5,2,2,2,2,2,128]{7,6,5,4,3,2,1,0:T(2,128)(2,1)} %param.11) | copy-start | bytes 614404
  3.5 0.9 %copy-start.3 = (f32[3,5,5,2,2,128]{5,4,3,2,1,0:T(2,128)S(1)}, f32[3,5,5,2,2,128]{5,4,3,2,1,0:T(2,128)}, u32[]{:S(2)}) copy-start(f32[3,5,5,2,2,128]{5,4,3,2,1,0:T(2,128)} %param.7) | copy-start | bytes 460804
  4.4 0.7 %copy-start.4 = (s32[3,2,2,128]{3,2,1,0:T(2,128)S(1)}, s32[3,2,2,128]{3,2,1,0:T(2,128)}, u32[]{:S(2)}) copy-start(s32[3,2,2,128]{3,2,1,0:T(2,128)} %param.9) | copy-start | bytes 18436
  5.1 0.7 %copy-start.5 = (f32[2,2,128]{2,1,0:T(2,128)S(1)}, f32[2,2,128]{2,1,0:T(2,128)}, u32[]{:S(2)}) copy-start(f32[2,2,128]{2,1,0:T(2,128)} %param.8) | copy-start | bytes 6148
where the time goes:
time: 40.8 us; the launch traced here: 40.6 us
  Pallas kernels  34 us (83%)
  local copies, waits for them, and re-layouts  6.57 us (16%)
    pallas_call x1, Pallas kernels, body(): pl.pallas_call(kernel, out_shape=jax.ShapeDtypeStruct(field, F32), in_spe...  34 us
    unnamed x13, local copies, waits for them, and re-layouts  6.57 us

commit v1 on v0

--- a/solution.py
+++ b/solution.py
@@ -591,7 +591,7 @@
             pltpu.SemaphoreType.DMA((16,)),
         ],
         compiler_params=pltpu.CompilerParams(
-            collective_id=0, has_side_effects=True, vmem_limit_bytes=40 * 1024 * 1024
+            collective_id=0, has_side_effects=True
         ),
     )(
         source.reshape(field),

time: 40.8 us -> 36.2 us (0.89)
  local copies, waits for them, and re-layouts: 6.57 us -> 2.25 us
    unnamed x13 -> x1, local copies, waits for them, and re-layouts: 6.57 us -> 2.25 us
where the time goes in v1:
time: 36.2 us; the launch traced here: 36.1 us
  Pallas kernels  33.8 us (93%)
  local copies, waits for them, and re-layouts  2.25 us (6%)
    pallas_call x1, Pallas kernels, body(): pl.pallas_call(kernel, out_shape=jax.ShapeDtypeStruct(field, F32), in_spe...  33.8 us
    unnamed x1, local copies, waits for them, and re-layouts  2.25 us

profile of v1, /device:TPU:56, one launch (start us, length us, event | category | flops | bytes accessed | tf_op | source)
XLA Modules:
  0.0 36.1 jit_solution(2093408293692274819)
XLA Ops:
  0.0 33.8 %shard_map.64 = f32[5,4,4,2,8,128]{5,4,3,2,1,0:T(8,128)} custom-call(f32[5,4,4,2,8,128]{5,4,3,2,1,0:T(8,128)} %bitcast.9, f32[75,4,128]{2,1,0:T(4,128)} %bitcast.11, f32[4,128]{1,0:T(4,128)} %bitcast.13, s32[3,4,128]{2,1,0:T(4,128)} %bitcast.12, bf16[25,4,4,16,128]{4,3,2,1,0:T(8,128)(2,1)} %bitcast.8, bf16[25,2,16,128]{3,2,1,0:T(8,128)(2,1)} %bitcast.10), custom_call_target="tpu_custom_call" | custom-call | tf_op jit(solution)/shard_map/pallas_call | solution.py:556
  33.8 2.2 %copy.8 = f32[5,4,4,4,2,2,128]{6,5,4,3,2,1,0:T(2,128)} copy(f32[5,4,4,4,2,2,128]{6,5,4,3,2,1,0:T(2,128)} %bitcast.7) | data formatting | bytes 1310720

commit v2 on v1

--- a/solution.py
+++ b/solution.py
@@ -109,17 +109,26 @@
     ]
 
 
+def swap_rows(value, step):
+    return jnp.where((rows() & step) == 0, sub_roll(value, -step), sub_roll(value, step))
+
+
 def kernel(
-    src_hbm, jac_hbm, damp_hbm, flag_hbm, smo_hbm, csm_hbm, out_hbm,
-    src, smo, csm, jraw, jn, draw, fraw, flags, dmp, kfine, csf,
-    q, acc, wx, wy, wz, rsrc, rcs, ctr, wc, cfield, crhs,
-    s1, r1, s2, r2, in_sem, out_sem, send_sem, recv_sem,
+    src_hbm, jac_hbm, damp_hbm, flag_hbm, smo_hbm, csm_hbm, out,
+    src, smo, csm, jraw, jn, draw, fraw, flags, dmp, kfine, csf, kface,
+    q, acc, wx, wy, wz, rsrc, rcs, ctr, wc, cfield, crhs, gcor,
+    s1, r1, s2, r2, s3, r3, sp, rp, sd, rd, sg, rg, in_sem, send_sem, recv_sem,
 ):
     nx, ny = lax.axis_size("gx"), lax.axis_size("gy")
     ix, iy = lax.axis_index("gx"), lax.axis_index("gy")
     x_next, x_prev = lax.rem(ix + 1, nx), lax.rem(ix + nx - 1, nx)
     y_next, y_prev = lax.rem(iy + 1, ny), lax.rem(iy + ny - 1, ny)
     partners = [(x_prev, iy), (x_next, iy), (ix, y_prev), (ix, y_next)]
+    corners = [(x_prev, y_prev), (x_next, y_prev), (x_prev, y_next), (x_next, y_next)]
+
+    barrier = pltpu.get_barrier_semaphore()
+    for partner in partners + corners:
+        pl.semaphore_signal(barrier, inc=1, device_id=partner, device_id_type=MESH)
 
     loads = []
 
@@ -135,29 +144,31 @@
     flag_load = load(flag_hbm, fraw)
     damp_load = load(damp_hbm, draw)
     jac_load = load(jac_hbm, jraw)
+    csm_load = load(csm_hbm, csm)
     for a in (1, 2):
         parts[a] = (load(src_hbm.at[:, a], src.at[:, a]), load(smo_hbm.at[:, a], smo.at[:, a]))
-    csm_load = load(csm_hbm, csm)
-
-    barrier = pltpu.get_barrier_semaphore()
-    for partner in partners:
-        pl.semaphore_signal(barrier, inc=1, device_id=partner, device_id_type=MESH)
+
+    started = []
 
     def remote(source, target, number, partner):
-        return pltpu.make_async_remote_copy(
+        copy = pltpu.make_async_remote_copy(
             src_ref=source, dst_ref=target, send_sem=send_sem.at[number], recv_sem=recv_sem.at[number],
             device_id=partner, device_id_type=MESH,
         )
+        started.append(copy)
+        return copy
 
     sends1 = [remote(s1.at[k], r1.at[k], k, partners[k]) for k in range(4)]
-    sends2 = [[remote(s2.at[r, k], r2.at[r, k], 4 + 4 * r + k, partners[k]) for k in range(4)] for r in range(3)]
+    sends2 = [remote(s2.at[k], r2.at[k], 4 + k, partners[k]) for k in range(4)]
+    sends3 = [remote(s3.at[k], r3.at[k], 8 + k, partners[k]) for k in range(4)]
+    sends_part = [remote(sp.at[k], rp.at[k], 12 + k, partners[k]) for k in range(4)]
+    sends_corner = [remote(sd.at[k], rd.at[k], 16 + k, corners[k]) for k in range(4)]
+    sends_face = [remote(sg.at[k], rg.at[k], 20 + k, partners[k]) for k in range(4)]
 
     low = rows() < 4
     x0 = (rows() & 2) == 0
     y0 = (rows() & 1) == 0
-
-    def turned(direction):
-        return flags[direction] == 1
+    zero = jnp.zeros((8, 128), F32)
 
     def smooth(a, b, fields):
         outs = []
@@ -190,6 +201,37 @@
     damp_load.wait()
     for d in range(3):
         flags[d] = jnp.concatenate([fraw[d], fraw[d]], axis=0)
+    fx, fy, fz = (flags[d] == 1 for d in range(3))
+
+    @pl.loop(0, 5)
+    def _(v):
+        for b in range(4):
+            s1[0, v, b] = pack_low(q[v, 0, b, 0], q[v, 0, b, 1], x0, 2)
+            hi = [jnp.where(fx, q[v, 3, 3 - b, h], q[v, 3, b, h]) for h in range(2)]
+            s1[1, v, b] = pack_high(hi[0], hi[1], x0, 2)
+
+    pl.semaphore_wait(barrier, 8)
+    sends1[0].start()
+    sends1[1].start()
+
+    for a in (1, 2):
+        for copy in parts[a]:
+            copy.wait()
+
+        @pl.loop(0, 4)
+        def _(b, a=a):
+            first_pass(a, b)
+
+    @pl.loop(0, 5)
+    def _(v):
+        for a in range(4):
+            s1[2, v, a] = pack_low(q[v, a, 0, 0], q[v, a, 0, 1], y0, 1)
+            hi = [jnp.where(fy, q[v, 3 - a, 3, h], q[v, a, 3, h]) for h in range(2)]
+            s1[3, v, a] = pack_high(hi[0], hi[1], y0, 1)
+
+    sends1[2].start()
+    sends1[3].start()
+
     damping = jnp.concatenate([draw[...], draw[...]], axis=0)
     dmp[0] = (OMEGA * LIFT) * damping
     dmp[1] = (OMEGA * 0.5) * damping
@@ -203,37 +245,6 @@
             kfine[b, a_end, 0] = base + dmp[3]
             kfine[b, a_end, 1] = base + dmp[4]
 
-    fx, fy, fz = turned(0), turned(1), turned(2)
-
-    @pl.loop(0, 5)
-    def _(v):
-        for b in range(4):
-            s1[0, v, b] = pack_low(q[v, 0, b, 0], q[v, 0, b, 1], x0, 2)
-            hi = [jnp.where(fx, q[v, 3, 3 - b, h], q[v, 3, b, h]) for h in range(2)]
-            s1[1, v, b] = pack_high(hi[0], hi[1], x0, 2)
-
-    pl.semaphore_wait(barrier, 4)
-    sends1[0].start()
-    sends1[1].start()
-
-    for a in (1, 2):
-        for copy in parts[a]:
-            copy.wait()
-
-        @pl.loop(0, 4)
-        def _(b, a=a):
-            first_pass(a, b)
-
-    @pl.loop(0, 5)
-    def _(v):
-        for a in range(4):
-            s1[2, v, a] = pack_low(q[v, a, 0, 0], q[v, a, 0, 1], y0, 1)
-            hi = [jnp.where(fy, q[v, 3 - a, 3, h], q[v, a, 3, h]) for h in range(2)]
-            s1[3, v, a] = pack_high(hi[0], hi[1], y0, 1)
-
-    sends1[2].start()
-    sends1[3].start()
-
     jac_load.wait()
 
     @pl.loop(0, 75)
@@ -249,6 +260,49 @@
             block = csm[i, n].astype(F32)
             csf[i, n, 0] = block[:8]
             csf[i, n, 1] = block[8:]
+
+    half_damp, k_coarse, lift_damp = dmp[1], dmp[2], dmp[0]
+
+    def pack_side(side, first, second):
+        mask, step = (x0, 2) if side < 2 else (y0, 1)
+        return (pack_low if side % 2 == 0 else pack_high)(first, second, mask, step)
+
+    for side in range(4):
+        own, other = (0, 1) if side < 2 else (1, 0)
+        sign = -0.5 if side % 2 == 0 else 0.5
+        cross_sign = jnp.where(y0 if side < 2 else x0, -0.5, 0.5)
+
+        @pl.loop(0, 5)
+        def _(row, side=side, own=own, other=other, sign=sign, cross_sign=cross_sign):
+            for col in range(5):
+                diag = jnp.where(row == col, half_damp, zero)
+                face = diag + sign * jn[25 * own + 5 * row + col]
+                cross = diag + cross_sign * jn[25 * other + 5 * row + col]
+                kface[0, 5 * row + col] = pack_side(side, face, face)
+                kface[1, 5 * row + col] = pack_side(side, cross, cross)
+
+        @pl.loop(0, 5)
+        def _(vo, side=side):
+            blocks = []
+            for m in range(5):
+                if side < 2:
+                    pair = [csf[5 * vo + m, side, j] for j in range(2)]
+                else:
+                    pair = [csf[5 * vo + m, i, side - 2] for i in range(2)]
+                blocks.append(pack_side(side, pair[0], pair[1]))
+            for n in range(2):
+                for vi in range(5):
+                    total = blocks[0] * kface[n, vi]
+                    for m in range(1, 5):
+                        total = total + blocks[m] * kface[n, 5 * m + vi]
+                    sg[side, 25 * n + 5 * vo + vi] = total
+
+        for n, d in enumerate((own, other)):
+            flag = jnp.where(flags[d] == 1, 1.0, 0.0)
+            sg[side, 50 + n] = pack_side(side, flag, flag)
+
+    for copy in sends_face:
+        copy.start()
 
     c_first = [halves(OPEN[0, 1], OPEN[1, 0]), halves(OPEN[0, 2], OPEN[1, 3]), halves(OPEN[0, 3], OPEN[1, 2])]
     c_second = [halves(OPEN[2, 3], OPEN[3, 2]), halves(OPEN[2, 0], OPEN[3, 1]), halves(OPEN[2, 1], OPEN[3, 0])]
@@ -283,6 +337,32 @@
             for b in range(4):
                 wy[v, a, b, h] = dot_terms(OPEN[b], line)
 
+    def mix(pair, directions, last):
+        @pl.loop(0, 4)
+        def _(b):
+            total = [[[acc[v, a, b, h] for h in range(2)] for a in pair] for v in range(5)]
+            for d in directions:
+                w = (wx, wy, wz)[d]
+                for vi in range(5):
+                    flux = [[w[vi, a, b, h] for h in range(2)] for a in pair]
+                    for vo in range(5):
+                        weight = jn[25 * d + 5 * vo + vi]
+                        for n in range(2):
+                            for h in range(2):
+                                total[vo][n][h] = total[vo][n][h] + weight * flux[n][h]
+            for n, a in enumerate(pair):
+                if last:
+                    outs = smooth(a, b, [total[v][n] for v in range(5)])
+                for v in range(5):
+                    for h in range(2):
+                        if last:
+                            q[v, a, b, h] = q[v, a, b, h] + outs[v][h]
+                        else:
+                            acc[v, a, b, h] = total[v][n][h]
+
+    mix((0, 3), (2,), False)
+    mix((1, 2), (0, 2), False)
+
     @pl.loop(0, 5)
     def _(v):
         by_a = []
@@ -291,8 +371,6 @@
         for j in range(2):
             for i, value in enumerate(restrict_line([by_a[a][j] for a in range(4)])):
                 rsrc[v, i, j] = value
-
-    lift_damp = dmp[0]
 
     sends1[2].wait_recv()
     sends1[3].wait_recv()
@@ -316,6 +394,18 @@
                 acc[v, a, 0, h] = acc[v, a, 0, h] + lift_damp * left
                 acc[v, a, 3, h] = acc[v, a, 3, h] + lift_damp * ghost
 
+    mix((0, 3), (1,), False)
+    mix((1, 2), (1,), True)
+
+    def restrict_c_into(v, a_list):
+        for a in a_list:
+            for b in range(4):
+                rcs[v, a, b] = restrict_c(q[v, a, b, 0], q[v, a, b, 1])[3]
+
+    @pl.loop(0, 5)
+    def _(v):
+        restrict_c_into(v, (1, 2))
+
     sends1[0].wait_recv()
     sends1[1].wait_recv()
 
@@ -338,56 +428,41 @@
                 acc[v, 0, b, h] = acc[v, 0, b, h] + lift_damp * left
                 acc[v, 3, b, h] = acc[v, 3, b, h] + lift_damp * ghost
 
-    @pl.loop(0, 8)
-    def _(t):
-        half, b = t // 4, t % 4
-        pair = [half, 3 - half]
-        total = [[[acc[v, a, b, h] for h in range(2)] for a in pair] for v in range(5)]
-        for d, w in enumerate((wx, wy, wz)):
-            for vi in range(5):
-                flux = [[w[vi, a, b, h] for h in range(2)] for a in pair]
-                for vo in range(5):
-                    weight = jn[25 * d + 5 * vo + vi]
-                    for n in range(2):
-                        for h in range(2):
-                            total[vo][n][h] = total[vo][n][h] + weight * flux[n][h]
-        for n, a in enumerate(pair):
-            outs = smooth(a, b, [total[v][n] for v in range(5)])
-            for v in range(5):
-                for h in range(2):
-                    q[v, a, b, h] = q[v, a, b, h] + outs[v][h]
-
-    def send_coarse(level):
-        @pl.loop(0, 5)
-        def _(v):
-            s2[level, 0, v] = pack_low(ctr[0, v, 0], ctr[0, v, 1], x0, 2)
-            hi = [jnp.where(fx, ctr[1, v, 1 - j], ctr[1, v, j]) for j in range(2)]
-            s2[level, 1, v] = pack_high(hi[0], hi[1], x0, 2)
-            s2[level, 2, v] = pack_low(ctr[2, v, 0], ctr[2, v, 1], y0, 1)
-            hi = [jnp.where(fy, ctr[3, v, 1 - i], ctr[3, v, i]) for i in range(2)]
-            s2[level, 3, v] = pack_high(hi[0], hi[1], y0, 1)
-
-        for copy in sends2[level]:
-            copy.start()
-
-    def coarse_ghosts(level, v, slot, mask, step, flip):
+    mix((0, 3), (0,), True)
+
+    def pack_traces(v, target, turn):
+        for side in range(4):
+            pair = [ctr[side, v, n] for n in range(2)]
+            if turn and side % 2 == 1:
+                flip = fx if side < 2 else fy
+                pair = [jnp.where(flip, pair[1 - n], pair[n]) for n in range(2)]
+            target[side, v] = pack_side(side, pair[0], pair[1])
+
+    @pl.loop(0, 5)
+    def _(v):
+        restrict_c_into(v, (0, 3))
+        for slot, a in ((0, 0), (1, 3)):
+            for n, value in enumerate(restrict_line([rcs[v, a, b] for b in range(4)])):
+                ctr[slot, v, n] = value
+        for slot, b in ((2, 0), (3, 3)):
+            for n, value in enumerate(restrict_line([rcs[v, a, b] for a in range(4)])):
+                ctr[slot, v, n] = value
+        pack_traces(v, s2, True)
+
+    for copy in sends2:
+        copy.start()
+
+    def inner_ghosts(v, slot, mask, step, flip):
         lo = [ctr[slot, v, n] for n in range(2)]
         hi = [ctr[slot + 1, v, n] for n in range(2)]
-        packed_lo, packed_hi = r2[level, slot, v], r2[level, slot + 1, v]
-        right = [
-            jnp.where(mask, sub_roll(lo[0], -step), sub_roll(packed_lo, step)),
-            jnp.where(mask, sub_roll(lo[1], -step), packed_lo),
-        ]
+        right = [jnp.where(mask, sub_roll(value, -step), zero) for value in lo]
         right = [jnp.where(flip, right[1 - n], right[n]) for n in range(2)]
         hi = [jnp.where(flip, hi[1 - n], hi[n]) for n in range(2)]
-        left = [
-            jnp.where(mask, packed_hi, sub_roll(hi[0], step)),
-            jnp.where(mask, sub_roll(packed_hi, -step), sub_roll(hi[1], step)),
-        ]
+        left = [jnp.where(mask, zero, sub_roll(value, step)) for value in hi]
         return left, right
 
-    def coarse_mix():
-        total = [[[crhs[1, v, i, j] for j in range(2)] for i in range(2)] for v in range(5)]
+    def coarse_sweep():
+        total = [[[crhs[v, i, j] for j in range(2)] for i in range(2)] for v in range(5)]
         for d in range(3):
             for vi in range(5):
                 flux = [[wc[d, vi, i, j] for j in range(2)] for i in range(2)]
@@ -396,9 +471,6 @@
                     for i in range(2):
                         for j in range(2):
                             total[vo][i][j] = total[vo][i][j] + weight * flux[i][j]
-        return total
-
-    def coarse_smooth(total):
         outs = [[[None, None] for _ in range(2)] for _ in range(5)]
         for vo in range(5):
             for vi in range(5):
@@ -408,23 +480,6 @@
                         outs[vo][i][j] = term if vi == 0 else outs[vo][i][j] + term
         return outs
 
-    @pl.loop(0, 5)
-    def _(v):
-        rc = [[restrict_c(q[v, a, b, 0], q[v, a, b, 1])[3] for b in range(4)] for a in range(4)]
-        rbc = [restrict_line(rc[a]) for a in range(4)]
-        rac = [restrict_line([rc[a][b] for a in range(4)]) for b in range(4)]
-        for n in range(2):
-            ctr[0, v, n] = rbc[0][n]
-            ctr[1, v, n] = rbc[3][n]
-            ctr[2, v, n] = rac[0][n]
-            ctr[3, v, n] = rac[3][n]
-        for i in range(2):
-            for j in range(2):
-                wc[0, v, i, j] = dot_terms(EDGE[i], [rbc[a][j] for a in range(4)])
-                wc[1, v, i, j] = dot_terms(EDGE[j], [rac[b][i] for b in range(4)])
-
-    send_coarse(0)
-
     e_ends = halves(EDGE[0, 0], EDGE[1, 3])
     e_ends_sw = halves(EDGE[0, 3], EDGE[1, 0])
     e_inner = halves(EDGE[0, 1], EDGE[1, 2])
@@ -433,6 +488,12 @@
 
     @pl.loop(0, 5)
     def _(v):
+        rbc = [restrict_line([rcs[v, a, b] for b in range(4)]) for a in range(4)]
+        rac = [restrict_line([rcs[v, a, b] for a in range(4)]) for b in range(4)]
+        for i in range(2):
+            for j in range(2):
+                wc[0, v, i, j] = dot_terms(EDGE[i], [rbc[a][j] for a in range(4)])
+                wc[1, v, i, j] = dot_terms(EDGE[j], [rac[b][i] for b in range(4)])
         ra = [[restrict_line([q[v, a, b, h] for a in range(4)]) for b in range(4)] for h in range(2)]
         traces = [[None, None], [None, None]]
         for i in range(2):
@@ -444,120 +505,222 @@
                 wc[2, v, i, j] = (
                     e_ends * ends + e_ends_sw * sub_roll(ends, 4) + e_inner * inner + e_inner_sw * inner_sw
                 )
-                crhs[1, v, i, j] = rsrc[v, i, j] - (OMEGA * SHIFT) * full
+                crhs[v, i, j] = rsrc[v, i, j] - (OMEGA * SHIFT) * full
         for j in range(2):
             ghosts = z_ghosts(traces[j], fz)
             for i in range(2):
                 wc[2, v, i, j] = wc[2, v, i, j] + z_lift * ghosts[i]
-                crhs[1, v, i, j] = crhs[1, v, i, j] + lift_damp * (ghosts[i] - traces[j][i])
-
-    for copy in sends2[0]:
-        copy.wait_recv()
-
-    @pl.loop(0, 5)
-    def _(v):
-        left, right = coarse_ghosts(0, v, 0, x0, 2, fx)
+                crhs[v, i, j] = crhs[v, i, j] + lift_damp * (ghosts[i] - traces[j][i])
+
+    @pl.loop(0, 5)
+    def _(v):
+        left, right = inner_ghosts(v, 0, x0, 2, fx)
         for j in range(2):
             wc[0, v, 0, j] = wc[0, v, 0, j] - LIFT * left[j]
             wc[0, v, 1, j] = wc[0, v, 1, j] + LIFT * right[j]
-            crhs[1, v, 0, j] = crhs[1, v, 0, j] + lift_damp * (left[j] - ctr[0, v, j])
-            crhs[1, v, 1, j] = crhs[1, v, 1, j] + lift_damp * (right[j] - ctr[1, v, j])
-        left, right = coarse_ghosts(0, v, 2, y0, 1, fy)
+            crhs[v, 0, j] = crhs[v, 0, j] + lift_damp * (left[j] - ctr[0, v, j])
+            crhs[v, 1, j] = crhs[v, 1, j] + lift_damp * (right[j] - ctr[1, v, j])
+        left, right = inner_ghosts(v, 2, y0, 1, fy)
         for i in range(2):
             wc[1, v, i, 0] = wc[1, v, i, 0] - LIFT * left[i]
             wc[1, v, i, 1] = wc[1, v, i, 1] + LIFT * right[i]
-            crhs[1, v, i, 0] = crhs[1, v, i, 0] + lift_damp * (left[i] - ctr[2, v, i])
-            crhs[1, v, i, 1] = crhs[1, v, i, 1] + lift_damp * (right[i] - ctr[3, v, i])
-
-    total = coarse_mix()
+            crhs[v, i, 0] = crhs[v, i, 0] + lift_damp * (left[i] - ctr[2, v, i])
+            crhs[v, i, 1] = crhs[v, i, 1] + lift_damp * (right[i] - ctr[3, v, i])
+
+    outs = coarse_sweep()
     for v in range(5):
         for i in range(2):
             for j in range(2):
-                crhs[0, v, i, j] = total[v][i][j]
-    outs = coarse_smooth(total)
+                cfield[0, v, i, j] = outs[v][i][j]
+
+    @pl.loop(0, 20)
+    def _(t):
+        v, b = t // 4, t % 4
+        for a in range(4):
+            for h in range(2):
+                out[v, a, b, h] = OMEGA * q[v, a, b, h]
+
+    def face_product(ref, side, base, vectors):
+        outs = []
+        for vo in range(5):
+            total = ref[side, base + 5 * vo] * vectors[0]
+            for vi in range(1, 5):
+                total = total + ref[side, base + 5 * vo + vi] * vectors[vi]
+            outs.append(total)
+        return outs
+
+    def own_ghost(side, value):
+        if side % 2 == 0:
+            return value
+        return jnp.where(sg[side, 50] == 1.0, swap_rows(value, 2 if side < 2 else 1), value)
+
+    def add_faces(slot, scale, ghosts):
+        for side in range(4):
+            mask, step = (x0, 2) if side < 2 else (y0, 1)
+            for v, delta in enumerate(face_product(sg, side, 0, ghosts[side])):
+                if scale != 1.0:
+                    delta = scale * delta
+                if side % 2 == 0:
+                    pair = [jnp.where(mask, delta, zero), jnp.where(mask, sub_roll(delta, -step), zero)]
+                else:
+                    pair = [jnp.where(mask, zero, sub_roll(delta, step)), jnp.where(mask, zero, delta)]
+                for n in range(2):
+                    i, j = (side, n) if side < 2 else (n, side - 2)
+                    cfield[slot, v, i, j] = cfield[slot, v, i, j] + pair[n]
+
+    def inner_operator(slot):
+        @pl.loop(0, 5)
+        def _(v):
+            field = [[cfield[slot, v, i, j] for j in range(2)] for i in range(2)]
+            for n in range(2):
+                ctr[0, v, n] = field[0][n]
+                ctr[1, v, n] = field[1][n]
+                ctr[2, v, n] = field[n][0]
+                ctr[3, v, n] = field[n][1]
+            rhs = [[(-k_coarse) * field[i][j] for j in range(2)] for i in range(2)]
+            for j in range(2):
+                ghosts = z_ghosts([field[i][j] for i in range(2)], fz)
+                for i in range(2):
+                    swapped = sub_roll(field[i][j], 4)
+                    wc[2, v, i, j] = jnp.where(low, 0.5, -0.5) * (swapped - ghosts[i])
+                    rhs[i][j] = rhs[i][j] + half_damp * ghosts[i]
+            left, right = inner_ghosts(v, 0, x0, 2, fx)
+            for j in range(2):
+                wc[0, v, 0, j] = 0.5 * (field[1][j] - left[j])
+                wc[0, v, 1, j] = 0.5 * (right[j] - field[0][j])
+                rhs[0][j] = rhs[0][j] + half_damp * left[j]
+                rhs[1][j] = rhs[1][j] + half_damp * right[j]
+            left, right = inner_ghosts(v, 2, y0, 1, fy)
+            for i in range(2):
+                wc[1, v, i, 0] = 0.5 * (field[i][1] - left[i])
+                wc[1, v, i, 1] = 0.5 * (right[i] - field[i][0])
+                rhs[i][0] = rhs[i][0] + half_damp * left[i]
+                rhs[i][1] = rhs[i][1] + half_damp * right[i]
+            for i in range(2):
+                for j in range(2):
+                    crhs[v, i, j] = rhs[i][j]
+
+        return coarse_sweep()
+
+    for copy in sends2:
+        copy.wait_recv()
+    add_faces(0, 6.0, [[own_ghost(side, r2[side ^ 1, v]) for v in range(5)] for side in range(4)])
+
+    row4 = rows() & 3
+
+    @pl.loop(0, 5)
+    def _(v):
+        for n in range(2):
+            ctr[0, v, n] = cfield[0, v, 0, n]
+            ctr[1, v, n] = cfield[0, v, 1, n]
+            ctr[2, v, n] = cfield[0, v, n, 0]
+            ctr[3, v, n] = cfield[0, v, n, 1]
+        pack_traces(v, s3, True)
+        x_lo, x_hi, y_lo, y_hi = (s3[side, v] for side in range(4))
+        sd[0, v] = jnp.where(x0, y_lo, jnp.where(row4 == 2, x_lo, sub_roll(x_lo, 3)))
+        sd[1, v] = jnp.where(x0, x_hi, y_lo)
+        sd[2, v] = jnp.where(row4 == 0, y_hi, x_lo)
+        sd[3, v] = jnp.where(row4 == 3, y_hi, sub_roll(x_hi, -3))
+
+    for copy in sends3 + sends_corner:
+        copy.start()
+
+    outs = inner_operator(0)
     for v in range(5):
         for i in range(2):
             for j in range(2):
-                cfield[v, i, j] = outs[v][i][j]
-
-    half_damp, k_coarse = dmp[1], dmp[2]
-
-    for level in (1, 2):
-        @pl.loop(0, 5)
-        def _(v):
-            for n in range(2):
-                ctr[0, v, n] = cfield[v, 0, n]
-                ctr[1, v, n] = cfield[v, 1, n]
-                ctr[2, v, n] = cfield[v, n, 0]
-                ctr[3, v, n] = cfield[v, n, 1]
-
-        send_coarse(level)
-
-        @pl.loop(0, 5)
-        def _(v):
+                cfield[1, v, i, j] = 2.0 * cfield[0, v, i, j] + outs[v][i][j]
+
+    @pl.loop(0, 5)
+    def _(v):
+        for n in range(2):
+            ctr[0, v, n] = cfield[1, v, 0, n]
+            ctr[1, v, n] = cfield[1, v, 1, n]
+            ctr[2, v, n] = cfield[1, v, n, 0]
+            ctr[3, v, n] = cfield[1, v, n, 1]
+        pack_traces(v, sp, False)
+
+    for copy in sends_part:
+        copy.start()
+
+    for copy in sends_face + sends3 + sends_corner:
+        copy.wait_recv()
+
+    def corner_ghosts(side, v):
+        prev_prev, next_prev, prev_next, next_next = (rd[k, v] for k in (3, 2, 1, 0))
+        flip = rg[side ^ 1, 51] == 1.0
+        if side == 1:
+            lower = next_prev
+            upper = jnp.where(flip, sub_roll(next_next, 2), sub_roll(next_next, 3))
+        elif side == 0:
+            lower = sub_roll(prev_prev, -3)
+            upper = jnp.where(flip, sub_roll(prev_next, 1), prev_next)
+        elif side == 3:
+            lower = prev_next
+            upper = jnp.where(flip, sub_roll(next_next, 1), next_next)
+        else:
+            lower = prev_prev
+            upper = jnp.where(flip, sub_roll(next_prev, 2), next_prev)
+        return jnp.where(row4 == 0, lower, jnp.where(row4 == 3, upper, zero))
+
+    for side in range(4):
+        step = 2 if side < 2 else 1
+        mine = [s3[side, v] for v in range(5)]
+        if side % 2 == 0:
+            turn = rg[side ^ 1, 50] == 1.0
+            mine = [jnp.where(turn, swap_rows(value, step), value) for value in mine]
+        first = face_product(rg, side ^ 1, 0, mine)
+        second = face_product(rg, side ^ 1, 25, [corner_ghosts(side, v) for v in range(5)])
+        for v in range(5):
+            gcor[side, v] = first[v] + second[v]
+
+    add_faces(1, 1.0, [[own_ghost(side, r3[side ^ 1, v]) for v in range(5)] for side in range(4)])
+    outs = inner_operator(1)
+    for v in range(5):
+        for i in range(2):
             for j in range(2):
-                field = [cfield[v, i, j] for i in range(2)]
-                ghosts = z_ghosts(field, fz)
-                for i in range(2):
-                    swapped = sub_roll(field[i], 4)
-                    wc[2, v, i, j] = jnp.where(low, 0.5, -0.5) * (swapped - ghosts[i])
-                    crhs[1, v, i, j] = crhs[0, v, i, j] - k_coarse * field[i] + half_damp * ghosts[i]
-
-        for copy in sends2[level]:
-            copy.wait_recv()
-
-        @pl.loop(0, 5)
-        def _(v):
-            left, right = coarse_ghosts(level, v, 0, x0, 2, fx)
-            for j in range(2):
-                wc[0, v, 0, j] = 0.5 * (cfield[v, 1, j] - left[j])
-                wc[0, v, 1, j] = 0.5 * (right[j] - cfield[v, 0, j])
-                crhs[1, v, 0, j] = crhs[1, v, 0, j] + half_damp * left[j]
-                crhs[1, v, 1, j] = crhs[1, v, 1, j] + half_damp * right[j]
-            left, right = coarse_ghosts(level, v, 2, y0, 1, fy)
-            for i in range(2):
-                wc[1, v, i, 0] = 0.5 * (cfield[v, i, 1] - left[i])
-                wc[1, v, i, 1] = 0.5 * (right[i] - cfield[v, i, 0])
-                crhs[1, v, i, 0] = crhs[1, v, i, 0] + half_damp * left[i]
-                crhs[1, v, i, 1] = crhs[1, v, i, 1] + half_damp * right[i]
-
-        outs = coarse_smooth(coarse_mix())
-        for v in range(5):
-            for i in range(2):
-                for j in range(2):
-                    cfield[v, i, j] = cfield[v, i, j] + outs[v][i][j]
+                cfield[0, v, i, j] = cfield[0, v, i, j] + cfield[1, v, i, j] + outs[v][i][j]
+
+    for copy in sends_part:
+        copy.wait_recv()
+
+    ghosts = []
+    for side in range(4):
+        step = 2 if side < 2 else 1
+        values = [rp[side ^ 1, v] + gcor[side, v] for v in range(5)]
+        if side % 2 == 0:
+            turn = rg[side ^ 1, 50] == 1.0
+            values = [jnp.where(turn, swap_rows(value, step), value) for value in values]
+        else:
+            values = [own_ghost(side, value) for value in values]
+        ghosts.append(values)
+    add_faces(0, 1.0, ghosts)
 
     t_first = [halves(OMEGA, OMEGA * P_FAR), halves(0.0, OMEGA * P_NEAR)]
     t_second = [halves(OMEGA * P_FAR, OMEGA), halves(OMEGA * P_NEAR, 0.0)]
 
     @pl.loop(0, 5)
     def _(v):
-        by_a = [prolong_line([cfield[v, i, j] for i in range(2)]) for j in range(2)]
+        by_a = [prolong_line([cfield[0, v, i, j] for i in range(2)]) for j in range(2)]
         for a in range(4):
             for b, value in enumerate(prolong_line([by_a[j][a] for j in range(2)])):
                 swapped = sub_roll(value, 4)
-                wx[v, a, b, 0] = OMEGA * q[v, a, b, 0] + (t_first[0] * value + t_first[1] * swapped)
-                wx[v, a, b, 1] = OMEGA * q[v, a, b, 1] + (t_second[0] * value + t_second[1] * swapped)
-
-    store = pltpu.make_async_copy(wx, out_hbm, out_sem)
-    store.start()
-    for copy in sends1:
+                out[v, a, b, 0] = out[v, a, b, 0] + (t_first[0] * value + t_first[1] * swapped)
+                out[v, a, b, 1] = out[v, a, b, 1] + (t_second[0] * value + t_second[1] * swapped)
+
+    for copy in started:
         copy.wait_send()
-    for level in sends2:
-        for copy in level:
-            copy.wait_send()
-    store.wait()
 
 
 def body(source, jacobian, damping, orient, smoother, coarse_smoother):
     field = (5, 4, 4, 2, 8, 128)
-    any_space = pl.BlockSpec(memory_space=pl.ANY)
     vmem = pltpu.VMEM
+    hbm = pl.BlockSpec(memory_space=pltpu.HBM)
     out = pl.pallas_call(
         kernel,
-        out_shape=jax.ShapeDtypeStruct(field, F32),
-        in_specs=[any_space] * 6,
-        out_specs=any_space,
+        out_shape=pltpu.VMEM(field, F32),
+        in_specs=[hbm] * 6,
+        out_specs=pl.BlockSpec(memory_space=pltpu.VMEM),
         scratch_shapes=[
             vmem(field, F32),
             vmem((25, 4, 4, 16, 128), jnp.bfloat16),
@@ -570,29 +733,36 @@
             vmem((5, 8, 128), F32),
             vmem((4, 2, 2, 8, 128), F32),
             vmem((25, 2, 2, 8, 128), F32),
+            vmem((2, 25, 8, 128), F32),
             vmem(field, F32),
             vmem(field, F32),
             vmem(field, F32),
             vmem(field, F32),
             vmem(field, F32),
             vmem((5, 2, 2, 8, 128), F32),
-            vmem((8, 128), F32),
+            vmem((5, 4, 4, 8, 128), F32),
             vmem((4, 5, 2, 8, 128), F32),
             vmem((3, 5, 2, 2, 8, 128), F32),
+            vmem((2, 5, 2, 2, 8, 128), F32),
             vmem((5, 2, 2, 8, 128), F32),
-            vmem((2, 5, 2, 2, 8, 128), F32),
+            vmem((4, 5, 8, 128), F32),
             vmem((4, 5, 4, 8, 128), F32),
             vmem((4, 5, 4, 8, 128), F32),
-            vmem((3, 4, 5, 8, 128), F32),
-            vmem((3, 4, 5, 8, 128), F32),
+            vmem((4, 5, 8, 128), F32),
+            vmem((4, 5, 8, 128), F32),
+            vmem((4, 5, 8, 128), F32),
+            vmem((4, 5, 8, 128), F32),
+            vmem((4, 5, 8, 128), F32),
+            vmem((4, 5, 8, 128), F32),
+            vmem((4, 5, 8, 128), F32),
+            vmem((4, 5, 8, 128), F32),
+            vmem((4, 52, 8, 128), F32),
+            vmem((4, 52, 8, 128), F32),
             pltpu.SemaphoreType.DMA((12,)),
-            pltpu.SemaphoreType.DMA,
-            pltpu.SemaphoreType.DMA((16,)),
-            pltpu.SemaphoreType.DMA((16,)),
+            pltpu.SemaphoreType.DMA((24,)),
+            pltpu.SemaphoreType.DMA((24,)),
         ],
-        compiler_params=pltpu.CompilerParams(
-            collective_id=0, has_side_effects=True
-        ),
+        compiler_params=pltpu.CompilerParams(collective_id=0, has_side_effects=True),
     )(
         source.reshape(field),
         jacobian.reshape(75, 4, 128),

time: 36.2 us -> 32.5 us (0.90)
  the two profiles are of different devices: /device:TPU:56 before, /device:TPU:1 now
where the time goes in v2:
time: 32.5 us; the launch traced here: 32.4 us
  Pallas kernels  31.5 us (97%)
  local copies, waits for them, and re-layouts  0.84 us (3%)
    pallas_call x1, Pallas kernels, body(): pl.pallas_call(kernel, out_shape=pltpu.VMEM(field, F32), in_specs=[hbm] *...  31.5 us
    unnamed x1, local copies, waits for them, and re-layouts  0.84 us

profile of v2, /device:TPU:1, one launch (start us, length us, event | category | flops | bytes accessed | tf_op | source)
XLA Modules:
  0.0 32.4 jit_solution(15231033203778592110)
XLA Ops:
  0.0 31.5 %shard_map.64 = f32[5,4,4,2,8,128]{5,4,3,2,1,0:T(8,128)S(1)} custom-call(f32[5,4,4,2,8,128]{5,4,3,2,1,0:T(8,128)} %bitcast.9, f32[75,4,128]{2,1,0:T(4,128)} %bitcast.11, f32[4,128]{1,0:T(4,128)} %bitcast.13, s32[3,4,128]{2,1,0:T(4,128)} %bitcast.12, bf16[25,4,4,16,128]{4,3,2,1,0:T(8,128)(2,1)} %bitcast.8, bf16[25,2,16,128]{3,2,1,0:T(8,128)(2,1)} %bitcast.10), custom_call_target="tpu_custom_call" | custom-call | tf_op jit(solution)/shard_map/pallas_call | solution.py:719
  31.6 0.8 %copy.8 = f32[5,4,4,4,2,2,128]{6,5,4,3,2,1,0:T(2,128)} copy(f32[5,4,4,4,2,2,128]{6,5,4,3,2,1,0:T(2,128)S(1)} %bitcast.7) | data formatting | bytes 1310720

commit v3 on v2

--- a/solution.py
+++ b/solution.py
@@ -116,7 +116,7 @@
 def kernel(
     src_hbm, jac_hbm, damp_hbm, flag_hbm, smo_hbm, csm_hbm, out,
     src, smo, csm, jraw, jn, draw, fraw, flags, dmp, kfine, csf, kface,
-    q, acc, wx, wy, wz, rsrc, rcs, ctr, wc, cfield, crhs, gcor,
+    q, acc, wx, wy, wz, rsrc, rcs, cloc, cpart, gcor, wc, crhs,
     s1, r1, s2, r2, s3, r3, sp, rp, sd, rd, sg, rg, in_sem, send_sem, recv_sem,
 ):
     nx, ny = lax.axis_size("gx"), lax.axis_size("gy")
@@ -127,7 +127,7 @@
     corners = [(x_prev, y_prev), (x_next, y_prev), (x_prev, y_next), (x_next, y_next)]
 
     barrier = pltpu.get_barrier_semaphore()
-    for partner in partners + corners:
+    for partner in partners:
         pl.semaphore_signal(barrier, inc=1, device_id=partner, device_id_type=MESH)
 
     loads = []
@@ -139,13 +139,11 @@
         return copy
 
     parts = {}
-    for a in (0, 3):
-        parts[a] = (load(src_hbm.at[:, a], src.at[:, a]), load(smo_hbm.at[:, a], smo.at[:, a]))
     flag_load = load(flag_hbm, fraw)
     damp_load = load(damp_hbm, draw)
     jac_load = load(jac_hbm, jraw)
     csm_load = load(csm_hbm, csm)
-    for a in (1, 2):
+    for a in (0, 3, 1, 2):
         parts[a] = (load(src_hbm.at[:, a], src.at[:, a]), load(smo_hbm.at[:, a], smo.at[:, a]))
 
     started = []
@@ -169,6 +167,8 @@
     x0 = (rows() & 2) == 0
     y0 = (rows() & 1) == 0
     zero = jnp.zeros((8, 128), F32)
+    row4 = rows() & 3
+    edge_rows = jnp.logical_or(row4 == 0, row4 == 3)
 
     def smooth(a, b, fields):
         outs = []
@@ -189,49 +189,11 @@
             q[v, a, b, 0] = outs[v][0]
             q[v, a, b, 1] = outs[v][1]
 
-    for a in (0, 3):
-        for copy in parts[a]:
-            copy.wait()
-
-        @pl.loop(0, 4)
-        def _(b, a=a):
-            first_pass(a, b)
-
     flag_load.wait()
     damp_load.wait()
     for d in range(3):
         flags[d] = jnp.concatenate([fraw[d], fraw[d]], axis=0)
     fx, fy, fz = (flags[d] == 1 for d in range(3))
-
-    @pl.loop(0, 5)
-    def _(v):
-        for b in range(4):
-            s1[0, v, b] = pack_low(q[v, 0, b, 0], q[v, 0, b, 1], x0, 2)
-            hi = [jnp.where(fx, q[v, 3, 3 - b, h], q[v, 3, b, h]) for h in range(2)]
-            s1[1, v, b] = pack_high(hi[0], hi[1], x0, 2)
-
-    pl.semaphore_wait(barrier, 8)
-    sends1[0].start()
-    sends1[1].start()
-
-    for a in (1, 2):
-        for copy in parts[a]:
-            copy.wait()
-
-        @pl.loop(0, 4)
-        def _(b, a=a):
-            first_pass(a, b)
-
-    @pl.loop(0, 5)
-    def _(v):
-        for a in range(4):
-            s1[2, v, a] = pack_low(q[v, a, 0, 0], q[v, a, 0, 1], y0, 1)
-            hi = [jnp.where(fy, q[v, 3 - a, 3, h], q[v, a, 3, h]) for h in range(2)]
-            s1[3, v, a] = pack_high(hi[0], hi[1], y0, 1)
-
-    sends1[2].start()
-    sends1[3].start()
-
     damping = jnp.concatenate([draw[...], draw[...]], axis=0)
     dmp[0] = (OMEGA * LIFT) * damping
     dmp[1] = (OMEGA * 0.5) * damping
@@ -247,14 +209,14 @@
 
     jac_load.wait()
 
-    @pl.loop(0, 75)
+    @pl.loop(0, 75, unroll=15)
     def _(i):
         block = jraw[i]
         jn[i] = (-OMEGA) * jnp.concatenate([block, block], axis=0)
 
     csm_load.wait()
 
-    @pl.loop(0, 25)
+    @pl.loop(0, 25, unroll=5)
     def _(i):
         for n in range(2):
             block = csm[i, n].astype(F32)
@@ -272,7 +234,7 @@
         sign = -0.5 if side % 2 == 0 else 0.5
         cross_sign = jnp.where(y0 if side < 2 else x0, -0.5, 0.5)
 
-        @pl.loop(0, 5)
+        @pl.loop(0, 5, unroll=True)
         def _(row, side=side, own=own, other=other, sign=sign, cross_sign=cross_sign):
             for col in range(5):
                 diag = jnp.where(row == col, half_damp, zero)
@@ -281,7 +243,7 @@
                 kface[0, 5 * row + col] = pack_side(side, face, face)
                 kface[1, 5 * row + col] = pack_side(side, cross, cross)
 
-        @pl.loop(0, 5)
+        @pl.loop(0, 5, unroll=True)
         def _(vo, side=side):
             blocks = []
             for m in range(5):
@@ -290,16 +252,64 @@
                 else:
                     pair = [csf[5 * vo + m, i, side - 2] for i in range(2)]
                 blocks.append(pack_side(side, pair[0], pair[1]))
+            tiles = [[], []]
             for n in range(2):
                 for vi in range(5):
                     total = blocks[0] * kface[n, vi]
                     for m in range(1, 5):
                         total = total + blocks[m] * kface[n, 5 * m + vi]
-                    sg[side, 25 * n + 5 * vo + vi] = total
+                    tiles[n].append(total)
+            for vi in range(5):
+                sg[side, 5 * vo + vi] = tiles[0][vi]
+            for n in range(3):
+                tile = tiles[1][2 * n]
+                if n < 2:
+                    other = tiles[1][2 * n + 1]
+                    tile = jnp.where(
+                        edge_rows, tile, jnp.where(row4 == 1, sub_roll(other, 1), sub_roll(other, -1))
+                    )
+                sg[side, 25 + 3 * vo + n] = tile
 
         for n, d in enumerate((own, other)):
             flag = jnp.where(flags[d] == 1, 1.0, 0.0)
-            sg[side, 50 + n] = pack_side(side, flag, flag)
+            sg[side, 40 + n] = pack_side(side, flag, flag)
+
+    for a in (0, 3):
+        for copy in parts[a]:
+            copy.wait()
+
+        @pl.loop(0, 4)
+        def _(b, a=a):
+            first_pass(a, b)
+
+    @pl.loop(0, 5, unroll=True)
+    def _(v):
+        for b in range(4):
+            s1[0, v, b] = pack_low(q[v, 0, b, 0], q[v, 0, b, 1], x0, 2)
+            hi = [jnp.where(fx, q[v, 3, 3 - b, h], q[v, 3, b, h]) for h in range(2)]
+            s1[1, v, b] = pack_high(hi[0], hi[1], x0, 2)
+
+    pl.semaphore_wait(barrier, 4)
+    sends1[0].start()
+    sends1[1].start()
+
+    for a in (1, 2):
+        for copy in parts[a]:
+            copy.wait()
+
+        @pl.loop(0, 4)
+        def _(b, a=a):
+            first_pass(a, b)
+
+    @pl.loop(0, 5, unroll=True)
+    def _(v):
+        for a in range(4):
+            s1[2, v, a] = pack_low(q[v, a, 0, 0], q[v, a, 0, 1], y0, 1)
+            hi = [jnp.where(fy, q[v, 3 - a, 3, h], q[v, a, 3, h]) for h in range(2)]
+            s1[3, v, a] = pack_high(hi[0], hi[1], y0, 1)
+
+    sends1[2].start()
+    sends1[3].start()
 
     for copy in sends_face:
         copy.start()
@@ -308,7 +318,7 @@
     c_second = [halves(OPEN[2, 3], OPEN[3, 2]), halves(OPEN[2, 0], OPEN[3, 1]), halves(OPEN[2, 1], OPEN[3, 0])]
     c_ghost = [halves(-LIFT, 0.0), halves(0.0, LIFT)]
 
-    @pl.loop(0, 20)
+    @pl.loop(0, 20, unroll=4)
     def _(t):
         v, b = t // 4, t % 4
         first = [q[v, a, b, 0] for a in range(4)]
@@ -329,7 +339,7 @@
             acc[v, a, b, 0] = src[v, a, b, 0] - kfine[b, a_end, 0] * first[a] + dmp[3] * ghosts[a]
             acc[v, a, b, 1] = src[v, a, b, 1] - kfine[b, a_end, 1] * second[a] + dmp[4] * ghosts[a]
 
-    @pl.loop(0, 20)
+    @pl.loop(0, 20, unroll=4)
     def _(t):
         v, a = t // 4, t % 4
         for h in range(2):
@@ -363,7 +373,7 @@
     mix((0, 3), (2,), False)
     mix((1, 2), (0, 2), False)
 
-    @pl.loop(0, 5)
+    @pl.loop(0, 5, unroll=True)
     def _(v):
         by_a = []
         for a in range(4):
@@ -375,7 +385,7 @@
     sends1[2].wait_recv()
     sends1[3].wait_recv()
 
-    @pl.loop(0, 5)
+    @pl.loop(0, 5, unroll=True)
     def _(v):
         for h in range(2):
             lo = [q[v, a, 0, h] for a in range(4)]
@@ -402,14 +412,14 @@
             for b in range(4):
                 rcs[v, a, b] = restrict_c(q[v, a, b, 0], q[v, a, b, 1])[3]
 
-    @pl.loop(0, 5)
+    @pl.loop(0, 5, unroll=True)
     def _(v):
         restrict_c_into(v, (1, 2))
 
     sends1[0].wait_recv()
     sends1[1].wait_recv()
 
-    @pl.loop(0, 5)
+    @pl.loop(0, 5, unroll=True)
     def _(v):
         for h in range(2):
             lo = [q[v, 0, b, h] for b in range(4)]
@@ -430,31 +440,36 @@
 
     mix((0, 3), (0,), True)
 
-    def pack_traces(v, target, turn):
-        for side in range(4):
-            pair = [ctr[side, v, n] for n in range(2)]
-            if turn and side % 2 == 1:
-                flip = fx if side < 2 else fy
-                pair = [jnp.where(flip, pair[1 - n], pair[n]) for n in range(2)]
-            target[side, v] = pack_side(side, pair[0], pair[1])
-
-    @pl.loop(0, 5)
-    def _(v):
+    def traces_of(field):
+        return [
+            [[field[v][0][n] for n in range(2)] for v in range(5)],
+            [[field[v][1][n] for n in range(2)] for v in range(5)],
+            [[field[v][n][0] for n in range(2)] for v in range(5)],
+            [[field[v][n][1] for n in range(2)] for v in range(5)],
+        ]
+
+    def pack_traces(traces, target, turn):
+        for v in range(5):
+            for side in range(4):
+                pair = traces[side][v]
+                if turn and side % 2 == 1:
+                    flip = fx if side < 2 else fy
+                    pair = [jnp.where(flip, pair[1 - n], pair[n]) for n in range(2)]
+                target[side, v] = pack_side(side, pair[0], pair[1])
+
+    traces = [[None] * 5 for _ in range(4)]
+    for v in range(5):
         restrict_c_into(v, (0, 3))
         for slot, a in ((0, 0), (1, 3)):
-            for n, value in enumerate(restrict_line([rcs[v, a, b] for b in range(4)])):
-                ctr[slot, v, n] = value
+            traces[slot][v] = restrict_line([rcs[v, a, b] for b in range(4)])
         for slot, b in ((2, 0), (3, 3)):
-            for n, value in enumerate(restrict_line([rcs[v, a, b] for a in range(4)])):
-                ctr[slot, v, n] = value
-        pack_traces(v, s2, True)
+            traces[slot][v] = restrict_line([rcs[v, a, b] for a in range(4)])
+    pack_traces(traces, s2, True)
 
     for copy in sends2:
         copy.start()
 
-    def inner_ghosts(v, slot, mask, step, flip):
-        lo = [ctr[slot, v, n] for n in range(2)]
-        hi = [ctr[slot + 1, v, n] for n in range(2)]
+    def inner_ghosts(lo, hi, mask, step, flip):
         right = [jnp.where(mask, sub_roll(value, -step), zero) for value in lo]
         right = [jnp.where(flip, right[1 - n], right[n]) for n in range(2)]
         hi = [jnp.where(flip, hi[1 - n], hi[n]) for n in range(2)]
@@ -486,169 +501,190 @@
     e_inner_sw = halves(EDGE[0, 2], EDGE[1, 1])
     z_lift = halves(-LIFT, LIFT)
 
-    @pl.loop(0, 5)
-    def _(v):
+    for v in range(5):
         rbc = [restrict_line([rcs[v, a, b] for b in range(4)]) for a in range(4)]
         rac = [restrict_line([rcs[v, a, b] for a in range(4)]) for b in range(4)]
-        for i in range(2):
-            for j in range(2):
-                wc[0, v, i, j] = dot_terms(EDGE[i], [rbc[a][j] for a in range(4)])
-                wc[1, v, i, j] = dot_terms(EDGE[j], [rac[b][i] for b in range(4)])
         ra = [[restrict_line([q[v, a, b, h] for a in range(4)]) for b in range(4)] for h in range(2)]
-        traces = [[None, None], [None, None]]
+        ends_of = [[None, None], [None, None]]
+        rhs = [[None, None], [None, None]]
+        w = [[[None, None], [None, None]] for _ in range(3)]
         for i in range(2):
             first = restrict_line([ra[0][b][i] for b in range(4)])
             second = restrict_line([ra[1][b][i] for b in range(4)])
             for j in range(2):
+                w[0][i][j] = dot_terms(EDGE[i], [rbc[a][j] for a in range(4)])
+                w[1][i][j] = dot_terms(EDGE[j], [rac[b][i] for b in range(4)])
                 ends, inner, inner_sw, full = restrict_c(first[j], second[j])
-                traces[j][i] = ends
-                wc[2, v, i, j] = (
+                ends_of[j][i] = ends
+                w[2][i][j] = (
                     e_ends * ends + e_ends_sw * sub_roll(ends, 4) + e_inner * inner + e_inner_sw * inner_sw
                 )
-                crhs[v, i, j] = rsrc[v, i, j] - (OMEGA * SHIFT) * full
+                rhs[i][j] = rsrc[v, i, j] - (OMEGA * SHIFT) * full
         for j in range(2):
-            ghosts = z_ghosts(traces[j], fz)
+            ghosts = z_ghosts(ends_of[j], fz)
             for i in range(2):
-                wc[2, v, i, j] = wc[2, v, i, j] + z_lift * ghosts[i]
-                crhs[v, i, j] = crhs[v, i, j] + lift_damp * (ghosts[i] - traces[j][i])
-
-    @pl.loop(0, 5)
-    def _(v):
-        left, right = inner_ghosts(v, 0, x0, 2, fx)
+                w[2][i][j] = w[2][i][j] + z_lift * ghosts[i]
+                rhs[i][j] = rhs[i][j] + lift_damp * (ghosts[i] - ends_of[j][i])
+        left, right = inner_ghosts(traces[0][v], traces[1][v], x0, 2, fx)
         for j in range(2):
-            wc[0, v, 0, j] = wc[0, v, 0, j] - LIFT * left[j]
-            wc[0, v, 1, j] = wc[0, v, 1, j] + LIFT * right[j]
-            crhs[v, 0, j] = crhs[v, 0, j] + lift_damp * (left[j] - ctr[0, v, j])
-            crhs[v, 1, j] = crhs[v, 1, j] + lift_damp * (right[j] - ctr[1, v, j])
-        left, right = inner_ghosts(v, 2, y0, 1, fy)
+            w[0][0][j] = w[0][0][j] - LIFT * left[j]
+            w[0][1][j] = w[0][1][j] + LIFT * right[j]
+            rhs[0][j] = rhs[0][j] + lift_damp * (left[j] - traces[0][v][j])
+            rhs[1][j] = rhs[1][j] + lift_damp * (right[j] - traces[1][v][j])
+        left, right = inner_ghosts(traces[2][v], traces[3][v], y0, 1, fy)
         for i in range(2):
-            wc[1, v, i, 0] = wc[1, v, i, 0] - LIFT * left[i]
-            wc[1, v, i, 1] = wc[1, v, i, 1] + LIFT * right[i]
-            crhs[v, i, 0] = crhs[v, i, 0] + lift_damp * (left[i] - ctr[2, v, i])
-            crhs[v, i, 1] = crhs[v, i, 1] + lift_damp * (right[i] - ctr[3, v, i])
+            w[1][i][0] = w[1][i][0] - LIFT * left[i]
+            w[1][i][1] = w[1][i][1] + LIFT * right[i]
+            rhs[i][0] = rhs[i][0] + lift_damp * (left[i] - traces[2][v][i])
+            rhs[i][1] = rhs[i][1] + lift_damp * (right[i] - traces[3][v][i])
+        for i in range(2):
+            for j in range(2):
+                crhs[v, i, j] = rhs[i][j]
+                for d in range(3):
+                    wc[d, v, i, j] = w[d][i][j]
 
     outs = coarse_sweep()
     for v in range(5):
         for i in range(2):
             for j in range(2):
-                cfield[0, v, i, j] = outs[v][i][j]
-
-    @pl.loop(0, 20)
+                cloc[v, i, j] = outs[v][i][j]
+
+    @pl.loop(0, 20, unroll=4)
     def _(t):
         v, b = t // 4, t % 4
         for a in range(4):
             for h in range(2):
                 out[v, a, b, h] = OMEGA * q[v, a, b, h]
 
-    def face_product(ref, side, base, vectors):
+    def face_product(ref, side, vectors):
         outs = []
         for vo in range(5):
-            total = ref[side, base + 5 * vo] * vectors[0]
+            total = ref[side, 5 * vo] * vectors[0]
             for vi in range(1, 5):
-                total = total + ref[side, base + 5 * vo + vi] * vectors[vi]
+                total = total + ref[side, 5 * vo + vi] * vectors[vi]
             outs.append(total)
+        return outs
+
+    def corner_product(ref, side, vectors):
+        moved = [jnp.where(edge_rows, zero, jnp.where(row4 == 1, sub_roll(x, 1), sub_roll(x, -1))) for x in vectors]
+        joined = [vectors[0] + moved[1], vectors[2] + moved[3], vectors[4]]
+        outs = []
+        for vo in range(5):
+            total = ref[side, 25 + 3 * vo] * joined[0]
+            for n in range(1, 3):
+                total = total + ref[side, 25 + 3 * vo + n] * joined[n]
+            back = total + jnp.where(row4 == 0, sub_roll(total, -1), sub_roll(total, 1))
+            outs.append(jnp.where(edge_rows, back, zero))
         return outs
 
     def own_ghost(side, value):
         if side % 2 == 0:
             return value
-        return jnp.where(sg[side, 50] == 1.0, swap_rows(value, 2 if side < 2 else 1), value)
-
-    def add_faces(slot, scale, ghosts):
+        return jnp.where(sg[side, 40] == 1.0, swap_rows(value, 2 if side < 2 else 1), value)
+
+    def face_terms(ghosts):
+        pairs = [[None] * 5 for _ in range(4)]
         for side in range(4):
             mask, step = (x0, 2) if side < 2 else (y0, 1)
-            for v, delta in enumerate(face_product(sg, side, 0, ghosts[side])):
-                if scale != 1.0:
-                    delta = scale * delta
+            for v, delta in enumerate(face_product(sg, side, ghosts[side])):
                 if side % 2 == 0:
-                    pair = [jnp.where(mask, delta, zero), jnp.where(mask, sub_roll(delta, -step), zero)]
+                    pairs[side][v] = [
+                        jnp.where(mask, delta, zero), jnp.where(mask, sub_roll(delta, -step), zero)
+                    ]
                 else:
-                    pair = [jnp.where(mask, zero, sub_roll(delta, step)), jnp.where(mask, zero, delta)]
-                for n in range(2):
-                    i, j = (side, n) if side < 2 else (n, side - 2)
-                    cfield[slot, v, i, j] = cfield[slot, v, i, j] + pair[n]
-
-    def inner_operator(slot):
-        @pl.loop(0, 5)
-        def _(v):
-            field = [[cfield[slot, v, i, j] for j in range(2)] for i in range(2)]
-            for n in range(2):
-                ctr[0, v, n] = field[0][n]
-                ctr[1, v, n] = field[1][n]
-                ctr[2, v, n] = field[n][0]
-                ctr[3, v, n] = field[n][1]
-            rhs = [[(-k_coarse) * field[i][j] for j in range(2)] for i in range(2)]
+                    pairs[side][v] = [
+                        jnp.where(mask, zero, sub_roll(delta, step)), jnp.where(mask, zero, delta)
+                    ]
+        return [[[pairs[i][v][j] + pairs[2 + j][v][i] for j in range(2)] for i in range(2)] for v in range(5)]
+
+    def inner_operator(field):
+        for v in range(5):
+            here = field[v]
+            rhs = [[(-k_coarse) * here[i][j] for j in range(2)] for i in range(2)]
             for j in range(2):
-                ghosts = z_ghosts([field[i][j] for i in range(2)], fz)
+                ghosts = z_ghosts([here[i][j] for i in range(2)], fz)
                 for i in range(2):
-                    swapped = sub_roll(field[i][j], 4)
+                    swapped = sub_roll(here[i][j], 4)
                     wc[2, v, i, j] = jnp.where(low, 0.5, -0.5) * (swapped - ghosts[i])
                     rhs[i][j] = rhs[i][j] + half_damp * ghosts[i]
-            left, right = inner_ghosts(v, 0, x0, 2, fx)
+            left, right = inner_ghosts(here[0], here[1], x0, 2, fx)
             for j in range(2):
-                wc[0, v, 0, j] = 0.5 * (field[1][j] - left[j])
-                wc[0, v, 1, j] = 0.5 * (right[j] - field[0][j])
+                wc[0, v, 0, j] = 0.5 * (here[1][j] - left[j])
+                wc[0, v, 1, j] = 0.5 * (right[j] - here[0][j])
                 rhs[0][j] = rhs[0][j] + half_damp * left[j]
                 rhs[1][j] = rhs[1][j] + half_damp * right[j]
-            left, right = inner_ghosts(v, 2, y0, 1, fy)
+            left, right = inner_ghosts([here[i][0] for i in range(2)], [here[i][1] for i in range(2)], y0, 1, fy)
             for i in range(2):
-                wc[1, v, i, 0] = 0.5 * (field[i][1] - left[i])
-                wc[1, v, i, 1] = 0.5 * (right[i] - field[i][0])
+                wc[1, v, i, 0] = 0.5 * (here[i][1] - left[i])
+                wc[1, v, i, 1] = 0.5 * (right[i] - here[i][0])
                 rhs[i][0] = rhs[i][0] + half_damp * left[i]
                 rhs[i][1] = rhs[i][1] + half_damp * right[i]
             for i in range(2):
                 for j in range(2):
                     crhs[v, i, j] = rhs[i][j]
-
         return coarse_sweep()
+
+    def combine(function, *fields):
+        return [
+            [[function(*(f[v][i][j] for f in fields)) for j in range(2)] for i in range(2)] for v in range(5)
+        ]
+
+    def load_field(ref):
+        return [[[ref[v, i, j] for j in range(2)] for i in range(2)] for v in range(5)]
 
     for copy in sends2:
         copy.wait_recv()
-    add_faces(0, 6.0, [[own_ghost(side, r2[side ^ 1, v]) for v in range(5)] for side in range(4)])
-
-    row4 = rows() & 3
-
-    @pl.loop(0, 5)
-    def _(v):
-        for n in range(2):
-            ctr[0, v, n] = cfield[0, v, 0, n]
-            ctr[1, v, n] = cfield[0, v, 1, n]
-            ctr[2, v, n] = cfield[0, v, n, 0]
-            ctr[3, v, n] = cfield[0, v, n, 1]
-        pack_traces(v, s3, True)
+    terms = face_terms([[own_ghost(side, r2[side ^ 1, v]) for v in range(5)] for side in range(4)])
+    coarse = combine(lambda x, y: x + 6.0 * y, load_field(cloc), terms)
+    pack_traces(traces_of(coarse), s3, True)
+    for v in range(5):
         x_lo, x_hi, y_lo, y_hi = (s3[side, v] for side in range(4))
         sd[0, v] = jnp.where(x0, y_lo, jnp.where(row4 == 2, x_lo, sub_roll(x_lo, 3)))
         sd[1, v] = jnp.where(x0, x_hi, y_lo)
         sd[2, v] = jnp.where(row4 == 0, y_hi, x_lo)
         sd[3, v] = jnp.where(row4 == 3, y_hi, sub_roll(x_hi, -3))
 
-    for copy in sends3 + sends_corner:
+    for copy in sends_corner + sends3:
         copy.start()
 
-    outs = inner_operator(0)
+    outs = inner_operator(coarse)
+    partial = combine(lambda x, y: 2.0 * x + y, coarse, outs)
+    pack_traces(traces_of(partial), sp, False)
+
+    for copy in sends_part:
+        copy.start()
+
     for v in range(5):
         for i in range(2):
             for j in range(2):
-                cfield[1, v, i, j] = 2.0 * cfield[0, v, i, j] + outs[v][i][j]
-
-    @pl.loop(0, 5)
-    def _(v):
-        for n in range(2):
-            ctr[0, v, n] = cfield[1, v, 0, n]
-            ctr[1, v, n] = cfield[1, v, 1, n]
-            ctr[2, v, n] = cfield[1, v, n, 0]
-            ctr[3, v, n] = cfield[1, v, n, 1]
-        pack_traces(v, sp, False)
-
-    for copy in sends_part:
-        copy.start()
-
-    for copy in sends_face + sends3 + sends_corner:
+                cloc[v, i, j] = coarse[v][i][j]
+                cpart[v, i, j] = partial[v][i][j]
+
+    for copy in sends_face:
+        copy.wait_recv()
+
+    for side in range(4):
+        mine = [s3[side, v] for v in range(5)]
+        if side % 2 == 0:
+            turn = rg[side ^ 1, 40] == 1.0
+            mine = [jnp.where(turn, swap_rows(value, 2 if side < 2 else 1), value) for value in mine]
+        for v, value in enumerate(face_product(rg, side ^ 1, mine)):
+            gcor[side, v] = value
+
+    for copy in sends3:
+        copy.wait_recv()
+
+    terms = face_terms([[own_ghost(side, r3[side ^ 1, v]) for v in range(5)] for side in range(4)])
+    middle = combine(lambda x, y: x + y, load_field(cpart), terms)
+    outs = inner_operator(middle)
+    coarse = combine(lambda x, y, z: x + y + z, load_field(cloc), middle, outs)
+
+    for copy in sends_corner:
         copy.wait_recv()
 
     def corner_ghosts(side, v):
         prev_prev, next_prev, prev_next, next_next = (rd[k, v] for k in (3, 2, 1, 0))
-        flip = rg[side ^ 1, 51] == 1.0
+        flip = rg[side ^ 1, 41] == 1.0
         if side == 1:
             lower = next_prev
             upper = jnp.where(flip, sub_roll(next_next, 2), sub_roll(next_next, 3))
@@ -663,45 +699,27 @@
             upper = jnp.where(flip, sub_roll(next_prev, 2), next_prev)
         return jnp.where(row4 == 0, lower, jnp.where(row4 == 3, upper, zero))
 
-    for side in range(4):
-        step = 2 if side < 2 else 1
-        mine = [s3[side, v] for v in range(5)]
-        if side % 2 == 0:
-            turn = rg[side ^ 1, 50] == 1.0
-            mine = [jnp.where(turn, swap_rows(value, step), value) for value in mine]
-        first = face_product(rg, side ^ 1, 0, mine)
-        second = face_product(rg, side ^ 1, 25, [corner_ghosts(side, v) for v in range(5)])
-        for v in range(5):
-            gcor[side, v] = first[v] + second[v]
-
-    add_faces(1, 1.0, [[own_ghost(side, r3[side ^ 1, v]) for v in range(5)] for side in range(4)])
-    outs = inner_operator(1)
-    for v in range(5):
-        for i in range(2):
-            for j in range(2):
-                cfield[0, v, i, j] = cfield[0, v, i, j] + cfield[1, v, i, j] + outs[v][i][j]
+    beside = [corner_product(rg, side ^ 1, [corner_ghosts(side, v) for v in range(5)]) for side in range(4)]
 
     for copy in sends_part:
         copy.wait_recv()
 
     ghosts = []
     for side in range(4):
-        step = 2 if side < 2 else 1
-        values = [rp[side ^ 1, v] + gcor[side, v] for v in range(5)]
+        values = [rp[side ^ 1, v] + (gcor[side, v] + beside[side][v]) for v in range(5)]
         if side % 2 == 0:
-            turn = rg[side ^ 1, 50] == 1.0
-            values = [jnp.where(turn, swap_rows(value, step), value) for value in values]
+            turn = rg[side ^ 1, 40] == 1.0
+            values = [jnp.where(turn, swap_rows(value, 2 if side < 2 else 1), value) for value in values]
         else:
             values = [own_ghost(side, value) for value in values]
         ghosts.append(values)
-    add_faces(0, 1.0, ghosts)
+    coarse = combine(lambda x, y: x + y, coarse, face_terms(ghosts))
 
     t_first = [halves(OMEGA, OMEGA * P_FAR), halves(0.0, OMEGA * P_NEAR)]
     t_second = [halves(OMEGA * P_FAR, OMEGA), halves(OMEGA * P_NEAR, 0.0)]
 
-    @pl.loop(0, 5)
-    def _(v):
-        by_a = [prolong_line([cfield[0, v, i, j] for i in range(2)]) for j in range(2)]
+    for v in range(5):
+        by_a = [prolong_line([coarse[v][i][j] for i in range(2)]) for j in range(2)]
         for a in range(4):
             for b, value in enumerate(prolong_line([by_a[j][a] for j in range(2)])):
                 swapped = sub_roll(value, 4)
@@ -741,11 +759,11 @@
             vmem(field, F32),
             vmem((5, 2, 2, 8, 128), F32),
             vmem((5, 4, 4, 8, 128), F32),
-            vmem((4, 5, 2, 8, 128), F32),
-            vmem((3, 5, 2, 2, 8, 128), F32),
-            vmem((2, 5, 2, 2, 8, 128), F32),
+            vmem((5, 2, 2, 8, 128), F32),
             vmem((5, 2, 2, 8, 128), F32),
             vmem((4, 5, 8, 128), F32),
+            vmem((3, 5, 2, 2, 8, 128), F32),
+            vmem((5, 2, 2, 8, 128), F32),
             vmem((4, 5, 4, 8, 128), F32),
             vmem((4, 5, 4, 8, 128), F32),
             vmem((4, 5, 8, 128), F32),
@@ -756,8 +774,8 @@
             vmem((4, 5, 8, 128), F32),
             vmem((4, 5, 8, 128), F32),
             vmem((4, 5, 8, 128), F32),
-            vmem((4, 52, 8, 128), F32),
-            vmem((4, 52, 8, 128), F32),
+            vmem((4, 42, 8, 128), F32),
+            vmem((4, 42, 8, 128), F32),
             pltpu.SemaphoreType.DMA((12,)),
             pltpu.SemaphoreType.DMA((24,)),
             pltpu.SemaphoreType.DMA((24,)),

time: 32.5 us -> 30.6 us (0.942)
  Pallas kernels: 31.5 us -> 29.4 us
    pallas_call x1, Pallas kernels: 31.5 us -> 29.4 us  [body(): pl.pallas_call(kernel, out_shape=pltpu.VMEM(field, F32), in_specs=[hbm] *...]
where the time goes in v3:
time: 30.6 us; the launch traced here: 30.2 us
  Pallas kernels  29.4 us (96%)
  local copies, waits for them, and re-layouts  0.84 us (3%)
    pallas_call x1, Pallas kernels, body(): pl.pallas_call(kernel, out_shape=pltpu.VMEM(field, F32), in_specs=[hbm] *...  29.4 us
    unnamed x1, local copies, waits for them, and re-layouts  0.84 us

profile of v3, /device:TPU:1, one launch (start us, length us, event | category | flops | bytes accessed | tf_op | source)
XLA Modules:
  0.0 30.2 jit_solution(9380966094698493216)
XLA Ops:
  0.0 29.4 %shard_map.64 = f32[5,4,4,2,8,128]{5,4,3,2,1,0:T(8,128)S(1)} custom-call(f32[5,4,4,2,8,128]{5,4,3,2,1,0:T(8,128)} %bitcast.9, f32[75,4,128]{2,1,0:T(4,128)} %bitcast.11, f32[4,128]{1,0:T(4,128)} %bitcast.13, s32[3,4,128]{2,1,0:T(4,128)} %bitcast.12, bf16[25,4,4,16,128]{4,3,2,1,0:T(8,128)(2,1)} %bitcast.8, bf16[25,2,16,128]{3,2,1,0:T(8,128)(2,1)} %bitcast.10), custom_call_target="tpu_custom_call" | custom-call | tf_op jit(solution)/shard_map/pallas_call | solution.py:737
  29.4 0.8 %copy.8 = f32[5,4,4,4,2,2,128]{6,5,4,3,2,1,0:T(2,128)} copy(f32[5,4,4,4,2,2,128]{6,5,4,3,2,1,0:T(2,128)S(1)} %bitcast.7) | data formatting | bytes 1310720

commit v4 on v3

--- a/solution.py
+++ b/solution.py
@@ -109,6 +109,9 @@
     ]
 
 
+CORNERS = ((2, 0, 0, 0), (2, 1, 3, 0), (3, 0, 0, 3), (3, 1, 3, 3))
+
+
 def swap_rows(value, step):
     return jnp.where((rows() & step) == 0, sub_roll(value, -step), sub_roll(value, step))
 
@@ -156,19 +159,19 @@
         started.append(copy)
         return copy
 
-    sends1 = [remote(s1.at[k], r1.at[k], k, partners[k]) for k in range(4)]
-    sends2 = [remote(s2.at[k], r2.at[k], 4 + k, partners[k]) for k in range(4)]
-    sends3 = [remote(s3.at[k], r3.at[k], 8 + k, partners[k]) for k in range(4)]
-    sends_part = [remote(sp.at[k], rp.at[k], 12 + k, partners[k]) for k in range(4)]
-    sends_corner = [remote(sd.at[k], rd.at[k], 16 + k, corners[k]) for k in range(4)]
-    sends_face = [remote(sg.at[k], rg.at[k], 20 + k, partners[k]) for k in range(4)]
+    sends1 = [[remote(s1.at[k, h], r1.at[k, h], 2 * k + h, partners[k]) for h in range(2)] for k in range(2)]
+    sends1 += [[remote(s1.at[k], r1.at[k], 2 * k, partners[k])] for k in range(2, 4)]
+    sends2 = [remote(s2.at[k], r2.at[k], 8 + k, partners[k]) for k in range(4)]
+    sends3 = [remote(s3.at[k], r3.at[k], 12 + k, partners[k]) for k in range(4)]
+    sends_part = [remote(sp.at[k], rp.at[k], 16 + k, partners[k]) for k in range(4)]
+    sends_corner = [remote(sd.at[k], rd.at[k], 20 + k, corners[k]) for k in range(4)]
+    sends_face = [remote(sg.at[k], rg.at[k], 24 + k, partners[k]) for k in range(4)]
 
     low = rows() < 4
     x0 = (rows() & 2) == 0
     y0 = (rows() & 1) == 0
     zero = jnp.zeros((8, 128), F32)
     row4 = rows() & 3
-    edge_rows = jnp.logical_or(row4 == 0, row4 == 3)
 
     def smooth(a, b, fields):
         outs = []
@@ -230,18 +233,15 @@
         return (pack_low if side % 2 == 0 else pack_high)(first, second, mask, step)
 
     for side in range(4):
-        own, other = (0, 1) if side < 2 else (1, 0)
+        own = 0 if side < 2 else 1
         sign = -0.5 if side % 2 == 0 else 0.5
-        cross_sign = jnp.where(y0 if side < 2 else x0, -0.5, 0.5)
 
         @pl.loop(0, 5, unroll=True)
-        def _(row, side=side, own=own, other=other, sign=sign, cross_sign=cross_sign):
+        def _(row, side=side, own=own, sign=sign):
             for col in range(5):
                 diag = jnp.where(row == col, half_damp, zero)
                 face = diag + sign * jn[25 * own + 5 * row + col]
-                cross = diag + cross_sign * jn[25 * other + 5 * row + col]
-                kface[0, 5 * row + col] = pack_side(side, face, face)
-                kface[1, 5 * row + col] = pack_side(side, cross, cross)
+                kface[5 * row + col] = pack_side(side, face, face)
 
         @pl.loop(0, 5, unroll=True)
         def _(vo, side=side):
@@ -252,27 +252,14 @@
                 else:
                     pair = [csf[5 * vo + m, i, side - 2] for i in range(2)]
                 blocks.append(pack_side(side, pair[0], pair[1]))
-            tiles = [[], []]
-            for n in range(2):
-                for vi in range(5):
-                    total = blocks[0] * kface[n, vi]
-                    for m in range(1, 5):
-                        total = total + blocks[m] * kface[n, 5 * m + vi]
-                    tiles[n].append(total)
             for vi in range(5):
-                sg[side, 5 * vo + vi] = tiles[0][vi]
-            for n in range(3):
-                tile = tiles[1][2 * n]
-                if n < 2:
-                    other = tiles[1][2 * n + 1]
-                    tile = jnp.where(
-                        edge_rows, tile, jnp.where(row4 == 1, sub_roll(other, 1), sub_roll(other, -1))
-                    )
-                sg[side, 25 + 3 * vo + n] = tile
-
-        for n, d in enumerate((own, other)):
-            flag = jnp.where(flags[d] == 1, 1.0, 0.0)
-            sg[side, 40 + n] = pack_side(side, flag, flag)
+                total = blocks[0] * kface[vi]
+                for m in range(1, 5):
+                    total = total + blocks[m] * kface[5 * m + vi]
+                sg[side, 5 * vo + vi] = total
+
+        flag = jnp.where(flags[own] == 1, 1.0, 0.0)
+        sg[side, 25] = pack_side(side, flag, flag)
 
     for a in (0, 3):
         for copy in parts[a]:
@@ -282,16 +269,20 @@
         def _(b, a=a):
             first_pass(a, b)
 
+    HALF = {0: (0, 0), 3: (0, 1), 1: (1, 0), 2: (1, 1)}
+
     @pl.loop(0, 5, unroll=True)
     def _(v):
         for b in range(4):
-            s1[0, v, b] = pack_low(q[v, 0, b, 0], q[v, 0, b, 1], x0, 2)
+            half, place = HALF[b]
+            s1[0, half, v, place] = pack_low(q[v, 0, b, 0], q[v, 0, b, 1], x0, 2)
             hi = [jnp.where(fx, q[v, 3, 3 - b, h], q[v, 3, b, h]) for h in range(2)]
-            s1[1, v, b] = pack_high(hi[0], hi[1], x0, 2)
+            s1[1, half, v, place] = pack_high(hi[0], hi[1], x0, 2)
 
     pl.semaphore_wait(barrier, 4)
-    sends1[0].start()
-    sends1[1].start()
+    for half in range(2):
+        for k in range(2):
+            sends1[k][half].start()
 
     for a in (1, 2):
         for copy in parts[a]:
@@ -304,12 +295,12 @@
     @pl.loop(0, 5, unroll=True)
     def _(v):
         for a in range(4):
-            s1[2, v, a] = pack_low(q[v, a, 0, 0], q[v, a, 0, 1], y0, 1)
+            s1[2, a // 2, v, a % 2] = pack_low(q[v, a, 0, 0], q[v, a, 0, 1], y0, 1)
             hi = [jnp.where(fy, q[v, 3 - a, 3, h], q[v, a, 3, h]) for h in range(2)]
-            s1[3, v, a] = pack_high(hi[0], hi[1], y0, 1)
-
-    sends1[2].start()
-    sends1[3].start()
+            s1[3, a // 2, v, a % 2] = pack_high(hi[0], hi[1], y0, 1)
+
+    sends1[2][0].start()
+    sends1[3][0].start()
 
     for copy in sends_face:
         copy.start()
@@ -347,28 +338,31 @@
             for b in range(4):
                 wy[v, a, b, h] = dot_terms(OPEN[b], line)
 
+    def mix_at(b, pair, directions, last):
+        total = [[[acc[v, a, b, h] for h in range(2)] for a in pair] for v in range(5)]
+        for d in directions:
+            w = (wx, wy, wz)[d]
+            for vi in range(5):
+                flux = [[w[vi, a, b, h] for h in range(2)] for a in pair]
+                for vo in range(5):
+                    weight = jn[25 * d + 5 * vo + vi]
+                    for n in range(2):
+                        for h in range(2):
+                            total[vo][n][h] = total[vo][n][h] + weight * flux[n][h]
+        for n, a in enumerate(pair):
+            if last:
+                outs = smooth(a, b, [total[v][n] for v in range(5)])
+            for v in range(5):
+                for h in range(2):
+                    if last:
+                        q[v, a, b, h] = q[v, a, b, h] + outs[v][h]
+                    else:
+                        acc[v, a, b, h] = total[v][n][h]
+
     def mix(pair, directions, last):
         @pl.loop(0, 4)
         def _(b):
-            total = [[[acc[v, a, b, h] for h in range(2)] for a in pair] for v in range(5)]
-            for d in directions:
-                w = (wx, wy, wz)[d]
-                for vi in range(5):
-                    flux = [[w[vi, a, b, h] for h in range(2)] for a in pair]
-                    for vo in range(5):
-                        weight = jn[25 * d + 5 * vo + vi]
-                        for n in range(2):
-                            for h in range(2):
-                                total[vo][n][h] = total[vo][n][h] + weight * flux[n][h]
-            for n, a in enumerate(pair):
-                if last:
-                    outs = smooth(a, b, [total[v][n] for v in range(5)])
-                for v in range(5):
-                    for h in range(2):
-                        if last:
-                            q[v, a, b, h] = q[v, a, b, h] + outs[v][h]
-                        else:
-                            acc[v, a, b, h] = total[v][n][h]
+            mix_at(b, pair, directions, last)
 
     mix((0, 3), (2,), False)
     mix((1, 2), (0, 2), False)
@@ -382,8 +376,8 @@
             for i, value in enumerate(restrict_line([by_a[a][j] for a in range(4)])):
                 rsrc[v, i, j] = value
 
-    sends1[2].wait_recv()
-    sends1[3].wait_recv()
+    sends1[2][0].wait_recv()
+    sends1[3][0].wait_recv()
 
     @pl.loop(0, 5, unroll=True)
     def _(v):
@@ -392,10 +386,10 @@
             hi = [q[v, a, 3, h] for a in range(4)]
             right = []
             for a in range(4):
-                packed = r1[2, v, a]
+                packed = r1[2, a // 2, v, a % 2]
                 right.append(jnp.where(y0, sub_roll(lo[a], -1), sub_roll(packed, 1) if h == 0 else packed))
             for a in range(4):
-                packed = r1[3, v, a]
+                packed = r1[3, a // 2, v, a % 2]
                 hi_turned = jnp.where(fy, hi[3 - a], hi[a])
                 left = jnp.where(y0, packed if h == 0 else sub_roll(packed, -1), sub_roll(hi_turned, 1))
                 ghost = jnp.where(fy, right[3 - a], right[a])
@@ -416,29 +410,31 @@
     def _(v):
         restrict_c_into(v, (1, 2))
 
-    sends1[0].wait_recv()
-    sends1[1].wait_recv()
-
-    @pl.loop(0, 5, unroll=True)
-    def _(v):
-        for h in range(2):
-            lo = [q[v, 0, b, h] for b in range(4)]
-            hi = [q[v, 3, b, h] for b in range(4)]
-            right = []
-            for b in range(4):
-                packed = r1[0, v, b]
-                right.append(jnp.where(x0, sub_roll(lo[b], -2), sub_roll(packed, 2) if h == 0 else packed))
-            for b in range(4):
-                packed = r1[1, v, b]
-                hi_turned = jnp.where(fx, hi[3 - b], hi[b])
-                left = jnp.where(x0, packed if h == 0 else sub_roll(packed, -2), sub_roll(hi_turned, 2))
-                ghost = jnp.where(fx, right[3 - b], right[b])
-                wx[v, 0, b, h] = wx[v, 0, b, h] - LIFT * left
-                wx[v, 3, b, h] = wx[v, 3, b, h] + LIFT * ghost
-                acc[v, 0, b, h] = acc[v, 0, b, h] + lift_damp * left
-                acc[v, 3, b, h] = acc[v, 3, b, h] + lift_damp * ghost
-
-    mix((0, 3), (0,), True)
+    for half, nodes in enumerate(((0, 3), (1, 2))):
+        sends1[0][half].wait_recv()
+        sends1[1][half].wait_recv()
+
+        @pl.loop(0, 5, unroll=True)
+        def _(v, half=half, nodes=nodes):
+            for h in range(2):
+                lo = [q[v, 0, b, h] for b in nodes]
+                hi = [q[v, 3, b, h] for b in nodes]
+                right = []
+                for n in range(2):
+                    packed = r1[0, half, v, n]
+                    right.append(jnp.where(x0, sub_roll(lo[n], -2), sub_roll(packed, 2) if h == 0 else packed))
+                for n, b in enumerate(nodes):
+                    packed = r1[1, half, v, n]
+                    hi_turned = jnp.where(fx, hi[1 - n], hi[n])
+                    left = jnp.where(x0, packed if h == 0 else sub_roll(packed, -2), sub_roll(hi_turned, 2))
+                    ghost = jnp.where(fx, right[1 - n], right[n])
+                    wx[v, 0, b, h] = wx[v, 0, b, h] - LIFT * left
+                    wx[v, 3, b, h] = wx[v, 3, b, h] + LIFT * ghost
+                    acc[v, 0, b, h] = acc[v, 0, b, h] + lift_damp * left
+                    acc[v, 3, b, h] = acc[v, 3, b, h] + lift_damp * ghost
+
+        for b in nodes:
+            mix_at(b, (0, 3), (0,), True)
 
     def traces_of(field):
         return [
@@ -565,22 +561,10 @@
             outs.append(total)
         return outs
 
-    def corner_product(ref, side, vectors):
-        moved = [jnp.where(edge_rows, zero, jnp.where(row4 == 1, sub_roll(x, 1), sub_roll(x, -1))) for x in vectors]
-        joined = [vectors[0] + moved[1], vectors[2] + moved[3], vectors[4]]
-        outs = []
-        for vo in range(5):
-            total = ref[side, 25 + 3 * vo] * joined[0]
-            for n in range(1, 3):
-                total = total + ref[side, 25 + 3 * vo + n] * joined[n]
-            back = total + jnp.where(row4 == 0, sub_roll(total, -1), sub_roll(total, 1))
-            outs.append(jnp.where(edge_rows, back, zero))
-        return outs
-
     def own_ghost(side, value):
         if side % 2 == 0:
             return value
-        return jnp.where(sg[side, 40] == 1.0, swap_rows(value, 2 if side < 2 else 1), value)
+        return jnp.where(sg[side, 25] == 1.0, swap_rows(value, 2 if side < 2 else 1), value)
 
     def face_terms(ghosts):
         pairs = [[None] * 5 for _ in range(4)]
@@ -637,14 +621,30 @@
     terms = face_terms([[own_ghost(side, r2[side ^ 1, v]) for v in range(5)] for side in range(4)])
     coarse = combine(lambda x, y: x + 6.0 * y, load_field(cloc), terms)
     pack_traces(traces_of(coarse), s3, True)
-    for v in range(5):
-        x_lo, x_hi, y_lo, y_hi = (s3[side, v] for side in range(4))
-        sd[0, v] = jnp.where(x0, y_lo, jnp.where(row4 == 2, x_lo, sub_roll(x_lo, 3)))
-        sd[1, v] = jnp.where(x0, x_hi, y_lo)
-        sd[2, v] = jnp.where(row4 == 0, y_hi, x_lo)
-        sd[3, v] = jnp.where(row4 == 3, y_hi, sub_roll(x_hi, -3))
-
-    for copy in sends_corner + sends3:
+    for copy in sends3:
+        copy.start()
+
+    for copy in sends_face:
+        copy.wait_recv()
+
+    added = []
+    for side in range(4):
+        mine = [s3[side, v] for v in range(5)]
+        if side % 2 == 0:
+            turn = rg[side ^ 1, 25] == 1.0
+            mine = [jnp.where(turn, swap_rows(value, 2 if side < 2 else 1), value) for value in mine]
+        added.append(face_product(rg, side ^ 1, mine))
+    for k, (along_y, along_x, y_row, x_row) in enumerate(CORNERS):
+        slots = []
+        for v in range(5):
+            slots += [(added[along_y][v], y_row), (added[along_x][v], x_row)]
+        for n in range(3):
+            tile = zero
+            for place, (value, source) in enumerate(slots[4 * n : 4 * n + 4]):
+                tile = jnp.where(row4 == place, sub_roll(value, place - source), tile)
+            sd[k, n] = tile
+
+    for copy in sends_corner:
         copy.start()
 
     outs = inner_operator(coarse)
@@ -655,22 +655,13 @@
         copy.start()
 
     for v in range(5):
+        for side in range(4):
+            gcor[side, v] = added[side][v]
         for i in range(2):
             for j in range(2):
                 cloc[v, i, j] = coarse[v][i][j]
                 cpart[v, i, j] = partial[v][i][j]
 
-    for copy in sends_face:
-        copy.wait_recv()
-
-    for side in range(4):
-        mine = [s3[side, v] for v in range(5)]
-        if side % 2 == 0:
-            turn = rg[side ^ 1, 40] == 1.0
-            mine = [jnp.where(turn, swap_rows(value, 2 if side < 2 else 1), value) for value in mine]
-        for v, value in enumerate(face_product(rg, side ^ 1, mine)):
-            gcor[side, v] = value
-
     for copy in sends3:
         copy.wait_recv()
 
@@ -682,24 +673,14 @@
     for copy in sends_corner:
         copy.wait_recv()
 
-    def corner_ghosts(side, v):
-        prev_prev, next_prev, prev_next, next_next = (rd[k, v] for k in (3, 2, 1, 0))
-        flip = rg[side ^ 1, 41] == 1.0
-        if side == 1:
-            lower = next_prev
-            upper = jnp.where(flip, sub_roll(next_next, 2), sub_roll(next_next, 3))
-        elif side == 0:
-            lower = sub_roll(prev_prev, -3)
-            upper = jnp.where(flip, sub_roll(prev_next, 1), prev_next)
-        elif side == 3:
-            lower = prev_next
-            upper = jnp.where(flip, sub_roll(next_next, 1), next_next)
-        else:
-            lower = prev_prev
-            upper = jnp.where(flip, sub_roll(next_prev, 2), next_prev)
+    def corner_rows(side, v):
+        lower, upper = ((3, 1), (2, 0), (3, 2), (1, 0))[side]
+        slot = 2 * v + (0 if side < 2 else 1)
+        tile, place = slot // 4, slot % 4
+        lower, upper = sub_roll(rd[lower, tile], -place), sub_roll(rd[upper, tile], 3 - place)
         return jnp.where(row4 == 0, lower, jnp.where(row4 == 3, upper, zero))
 
-    beside = [corner_product(rg, side ^ 1, [corner_ghosts(side, v) for v in range(5)]) for side in range(4)]
+    beside = [[corner_rows(side, v) for v in range(5)] for side in range(4)]
 
     for copy in sends_part:
         copy.wait_recv()
@@ -708,7 +689,7 @@
     for side in range(4):
         values = [rp[side ^ 1, v] + (gcor[side, v] + beside[side][v]) for v in range(5)]
         if side % 2 == 0:
-            turn = rg[side ^ 1, 40] == 1.0
+            turn = rg[side ^ 1, 25] == 1.0
             values = [jnp.where(turn, swap_rows(value, 2 if side < 2 else 1), value) for value in values]
         else:
             values = [own_ghost(side, value) for value in values]
@@ -751,7 +732,7 @@
             vmem((5, 8, 128), F32),
             vmem((4, 2, 2, 8, 128), F32),
             vmem((25, 2, 2, 8, 128), F32),
-            vmem((2, 25, 8, 128), F32),
+            vmem((25, 8, 128), F32),
             vmem(field, F32),
             vmem(field, F32),
             vmem(field, F32),
@@ -764,21 +745,21 @@
             vmem((4, 5, 8, 128), F32),
             vmem((3, 5, 2, 2, 8, 128), F32),
             vmem((5, 2, 2, 8, 128), F32),
-            vmem((4, 5, 4, 8, 128), F32),
-            vmem((4, 5, 4, 8, 128), F32),
+            vmem((4, 2, 5, 2, 8, 128), F32),
+            vmem((4, 2, 5, 2, 8, 128), F32),
             vmem((4, 5, 8, 128), F32),
             vmem((4, 5, 8, 128), F32),
             vmem((4, 5, 8, 128), F32),
             vmem((4, 5, 8, 128), F32),
             vmem((4, 5, 8, 128), F32),
             vmem((4, 5, 8, 128), F32),
-            vmem((4, 5, 8, 128), F32),
-            vmem((4, 5, 8, 128), F32),
-            vmem((4, 42, 8, 128), F32),
-            vmem((4, 42, 8, 128), F32),
+            vmem((4, 3, 8, 128), F32),
+            vmem((4, 3, 8, 128), F32),
+            vmem((4, 26, 8, 128), F32),
+            vmem((4, 26, 8, 128), F32),
             pltpu.SemaphoreType.DMA((12,)),
-            pltpu.SemaphoreType.DMA((24,)),
-            pltpu.SemaphoreType.DMA((24,)),
+            pltpu.SemaphoreType.DMA((28,)),
+            pltpu.SemaphoreType.DMA((28,)),
         ],
         compiler_params=pltpu.CompilerParams(collective_id=0, has_side_effects=True),
     )(

time: 30.6 us -> 30.3 us (level)
  Pallas kernels: 29.4 us -> 29 us
    pallas_call x1, Pallas kernels: 29.4 us -> 29 us  [body(): pl.pallas_call(kernel, out_shape=pltpu.VMEM(field, F32), in_specs=[hbm] *...]
where the time goes in v4:
time: 30.3 us; the launch traced here: 29.9 us
  Pallas kernels  29 us (96%)
  local copies, waits for them, and re-layouts  0.84 us (3%)
    pallas_call x1, Pallas kernels, body(): pl.pallas_call(kernel, out_shape=pltpu.VMEM(field, F32), in_specs=[hbm] *...  29 us
    unnamed x1, local copies, waits for them, and re-layouts  0.84 us

profile of v4, /device:TPU:1, one launch (start us, length us, event | category | flops | bytes accessed | tf_op | source)
XLA Modules:
  0.0 29.9 jit_solution(6349643341998047991)
XLA Ops:
  0.0 29.0 %shard_map.64 = f32[5,4,4,2,8,128]{5,4,3,2,1,0:T(8,128)S(1)} custom-call(f32[5,4,4,2,8,128]{5,4,3,2,1,0:T(8,128)} %bitcast.9, f32[75,4,128]{2,1,0:T(4,128)} %bitcast.11, f32[4,128]{1,0:T(4,128)} %bitcast.13, s32[3,4,128]{2,1,0:T(4,128)} %bitcast.12, bf16[25,4,4,16,128]{4,3,2,1,0:T(8,128)(2,1)} %bitcast.8, bf16[25,2,16,128]{3,2,1,0:T(8,128)(2,1)} %bitcast.10), custom_call_target="tpu_custom_call" | custom-call | tf_op jit(solution)/shard_map/pallas_call | solution.py:718
  29.0 0.8 %copy.8 = f32[5,4,4,4,2,2,128]{6,5,4,3,2,1,0:T(2,128)} copy(f32[5,4,4,4,2,2,128]{6,5,4,3,2,1,0:T(2,128)S(1)} %bitcast.7) | data formatting | bytes 1310720

commit v5 on v4

--- a/solution.py
+++ b/solution.py
@@ -302,8 +302,6 @@
     sends1[2][0].start()
     sends1[3][0].start()
 
-    for copy in sends_face:
-        copy.start()
 
     c_first = [halves(OPEN[0, 1], OPEN[1, 0]), halves(OPEN[0, 2], OPEN[1, 3]), halves(OPEN[0, 3], OPEN[1, 2])]
     c_second = [halves(OPEN[2, 3], OPEN[3, 2]), halves(OPEN[2, 0], OPEN[3, 1]), halves(OPEN[2, 1], OPEN[3, 0])]
@@ -359,13 +357,16 @@
                     else:
                         acc[v, a, b, h] = total[v][n][h]
 
-    def mix(pair, directions, last):
-        @pl.loop(0, 4)
-        def _(b):
-            mix_at(b, pair, directions, last)
-
-    mix((0, 3), (2,), False)
-    mix((1, 2), (0, 2), False)
+    def mix(first, step, pair, directions, last):
+        @pl.loop(0, 2)
+        def _(t):
+            mix_at(first + step * t, pair, directions, last)
+
+    mix(0, 3, (0, 3), (2,), False)
+    mix(0, 3, (1, 2), (0, 2), False)
+
+    for copy in sends_face:
+        copy.start()
 
     @pl.loop(0, 5, unroll=True)
     def _(v):
@@ -375,6 +376,9 @@
         for j in range(2):
             for i, value in enumerate(restrict_line([by_a[a][j] for a in range(4)])):
                 rsrc[v, i, j] = value
+
+    mix(1, 1, (0, 3), (1, 2), False)
+    mix(1, 1, (1, 2), (0, 1, 2), True)
 
     sends1[2][0].wait_recv()
     sends1[3][0].wait_recv()
@@ -398,8 +402,8 @@
                 acc[v, a, 0, h] = acc[v, a, 0, h] + lift_damp * left
                 acc[v, a, 3, h] = acc[v, a, 3, h] + lift_damp * ghost
 
-    mix((0, 3), (1,), False)
-    mix((1, 2), (1,), True)
+    mix(0, 3, (0, 3), (1,), False)
+    mix(0, 3, (1, 2), (1,), True)
 
     def restrict_c_into(v, a_list):
         for a in a_list:

time: 30.3 us -> 29.9 us (0.987); the launches traced: 29.9 us -> 29.8 us
  no operation moved by 1% of the time
where the time goes in v5:
time: 29.9 us; the launch traced here: 29.8 us
  Pallas kernels  29 us (97%)
  local copies, waits for them, and re-layouts  0.84 us (3%)
    pallas_call x1, Pallas kernels, body(): pl.pallas_call(kernel, out_shape=pltpu.VMEM(field, F32), in_specs=[hbm] *...  29 us
    unnamed x1, local copies, waits for them, and re-layouts  0.84 us

profile of v5, /device:TPU:1, one launch (start us, length us, event | category | flops | bytes accessed | tf_op | source)
XLA Modules:
  0.0 29.8 jit_solution(7247899372801635513)
XLA Ops:
  0.0 29.0 %shard_map.64 = f32[5,4,4,2,8,128]{5,4,3,2,1,0:T(8,128)S(1)} custom-call(f32[5,4,4,2,8,128]{5,4,3,2,1,0:T(8,128)} %bitcast.9, f32[75,4,128]{2,1,0:T(4,128)} %bitcast.11, f32[4,128]{1,0:T(4,128)} %bitcast.13, s32[3,4,128]{2,1,0:T(4,128)} %bitcast.12, bf16[25,4,4,16,128]{4,3,2,1,0:T(8,128)(2,1)} %bitcast.8, bf16[25,2,16,128]{3,2,1,0:T(8,128)(2,1)} %bitcast.10), custom_call_target="tpu_custom_call" | custom-call | tf_op jit(solution)/shard_map/pallas_call | solution.py:722
  29.0 0.8 %copy.8 = f32[5,4,4,4,2,2,128]{6,5,4,3,2,1,0:T(2,128)} copy(f32[5,4,4,4,2,2,128]{6,5,4,3,2,1,0:T(2,128)S(1)} %bitcast.7) | data formatting | bytes 1310720

commit v6 on v5

--- a/solution.py
+++ b/solution.py
@@ -625,7 +625,7 @@
     terms = face_terms([[own_ghost(side, r2[side ^ 1, v]) for v in range(5)] for side in range(4)])
     coarse = combine(lambda x, y: x + 6.0 * y, load_field(cloc), terms)
     pack_traces(traces_of(coarse), s3, True)
-    for copy in sends3:
+    for copy in sends3[:2]:
         copy.start()
 
     for copy in sends_face:
@@ -648,7 +648,7 @@
                 tile = jnp.where(row4 == place, sub_roll(value, place - source), tile)
             sd[k, n] = tile
 
-    for copy in sends_corner:
+    for copy in sends_corner + sends3[2:]:
         copy.start()
 
     outs = inner_operator(coarse)

time: 29.9 us -> 29.9 us (level)
  no operation moved by 1% of the time
where the time goes in v6:
time: 29.9 us; the launch traced here: 29.8 us
  Pallas kernels  28.9 us (97%)
  local copies, waits for them, and re-layouts  0.84 us (3%)
    pallas_call x1, Pallas kernels, body(): pl.pallas_call(kernel, out_shape=pltpu.VMEM(field, F32), in_specs=[hbm] *...  28.9 us
    unnamed x1, local copies, waits for them, and re-layouts  0.84 us

profile of v6, /device:TPU:1, one launch (start us, length us, event | category | flops | bytes accessed | tf_op | source)
XLA Modules:
  0.0 29.8 jit_solution(14645902703207685389)
XLA Ops:
  0.0 28.9 %shard_map.64 = f32[5,4,4,2,8,128]{5,4,3,2,1,0:T(8,128)S(1)} custom-call(f32[5,4,4,2,8,128]{5,4,3,2,1,0:T(8,128)} %bitcast.9, f32[75,4,128]{2,1,0:T(4,128)} %bitcast.11, f32[4,128]{1,0:T(4,128)} %bitcast.13, s32[3,4,128]{2,1,0:T(4,128)} %bitcast.12, bf16[25,4,4,16,128]{4,3,2,1,0:T(8,128)(2,1)} %bitcast.8, bf16[25,2,16,128]{3,2,1,0:T(8,128)(2,1)} %bitcast.10), custom_call_target="tpu_custom_call" | custom-call | tf_op jit(solution)/shard_map/pallas_call | solution.py:722
  29.0 0.8 %copy.8 = f32[5,4,4,4,2,2,128]{6,5,4,3,2,1,0:T(2,128)} copy(f32[5,4,4,4,2,2,128]{6,5,4,3,2,1,0:T(2,128)S(1)} %bitcast.7) | data formatting | bytes 1310720

commit v7 on v6

--- a/solution.py
+++ b/solution.py
@@ -625,8 +625,6 @@
     terms = face_terms([[own_ghost(side, r2[side ^ 1, v]) for v in range(5)] for side in range(4)])
     coarse = combine(lambda x, y: x + 6.0 * y, load_field(cloc), terms)
     pack_traces(traces_of(coarse), s3, True)
-    for copy in sends3[:2]:
-        copy.start()
 
     for copy in sends_face:
         copy.wait_recv()
@@ -648,7 +646,7 @@
                 tile = jnp.where(row4 == place, sub_roll(value, place - source), tile)
             sd[k, n] = tile
 
-    for copy in sends_corner + sends3[2:]:
+    for copy in sends_corner + sends3:
         copy.start()
 
     outs = inner_operator(coarse)

time: 29.9 us -> 29.8 us (level)
  no operation moved by 1% of the time
where the time goes in v7:
time: 29.8 us; the launch traced here: 29.6 us
  Pallas kernels  28.8 us (97%)
  local copies, waits for them, and re-layouts  0.84 us (3%)
    pallas_call x1, Pallas kernels, body(): pl.pallas_call(kernel, out_shape=pltpu.VMEM(field, F32), in_specs=[hbm] *...  28.8 us
    unnamed x1, local copies, waits for them, and re-layouts  0.84 us

profile of v7, /device:TPU:1, one launch (start us, length us, event | category | flops | bytes accessed | tf_op | source)
XLA Modules:
  0.0 29.6 jit_solution(11298963660954777427)
XLA Ops:
  0.0 28.8 %shard_map.64 = f32[5,4,4,2,8,128]{5,4,3,2,1,0:T(8,128)S(1)} custom-call(f32[5,4,4,2,8,128]{5,4,3,2,1,0:T(8,128)} %bitcast.9, f32[75,4,128]{2,1,0:T(4,128)} %bitcast.11, f32[4,128]{1,0:T(4,128)} %bitcast.13, s32[3,4,128]{2,1,0:T(4,128)} %bitcast.12, bf16[25,4,4,16,128]{4,3,2,1,0:T(8,128)(2,1)} %bitcast.8, bf16[25,2,16,128]{3,2,1,0:T(8,128)(2,1)} %bitcast.10), custom_call_target="tpu_custom_call" | custom-call | tf_op jit(solution)/shard_map/pallas_call | solution.py:720
  28.8 0.8 %copy.8 = f32[5,4,4,4,2,2,128]{6,5,4,3,2,1,0:T(2,128)} copy(f32[5,4,4,4,2,2,128]{6,5,4,3,2,1,0:T(2,128)S(1)} %bitcast.7) | data formatting | bytes 1310720
